TPU v7x, 256 devices: a whole 4x4x8 slice. The times are simulated.
256 devices in a mesh: dp: 64 (over z, y_hi, x), hist: 4 (over y_lo, core).
Axes of the slice: x: 4, y: 4 (y_hi: 2, y_lo: 2; y = y_hi * 2 + y_lo), z: 8, core: 2. Of those that a mesh axis runs over, the one named last changes fastest.
Arguments:
- tokens: bfloat16 [64, 512, 512], P('dp', 'hist'), may hold values from -6 to 6
- targets: bfloat16 [64, 512, 512], P('dp', 'hist'), may hold values from -6 to 6
- target_ids: int32 [64, 512], P('dp', 'hist'), may hold values from 0 to 4095
- lengths: int32 [64], P('dp'), may hold values from 64 to 512
- negatives: bfloat16 [2048, 512], P('dp'), may hold values from -6 to 6
- negative_ids: int32 [2048], P('dp'), may hold values from 0 to 4095
- negative_counts: int32 [2048], P('dp'), may hold values from 1 to 64
- w_in: bfloat16 [512, 2048], replicated, may hold values from -0.25 to 0.25
- w_out: bfloat16 [512, 512], replicated, may hold values from -0.25 to 0.25
Outputs:
- loss: float32 [], replicated
- d_tokens: bfloat16 [64, 512, 512], P('dp', 'hist')
- d_targets: bfloat16 [64, 512, 512], P('dp', 'hist')
- d_w_in: float32 [512, 2048], P('dp')
- d_w_out: float32 [512, 512], P('dp')
- d_negatives: float32 [2048, 512], P('dp')
All inputs are finite; a program needn't handle non-finite values.
Results may differ from a plain program's by a relative error of at most 0.018.
Values may be sent and summed in bfloat16 or wider, within the bound.
A program may use at most 64 MiB of HBM per device.

v0:
```python
import jax
import jax.numpy as jnp
from jax import lax
from jax.sharding import PartitionSpec as P

HEADS = 8
L = 512


SOFTMAX_TEMP = 0.05


def layer_norm(values):
    centered = values - jnp.mean(values, -1, keepdims=True)
    inverse = lax.rsqrt(jnp.mean(centered * centered, -1, keepdims=True) + 1e-06)
    return (centered * inverse, inverse)


def norm_back(grad, normed, inverse):
    return inverse * (
        grad
        - jnp.mean(grad, -1, keepdims=True)
        - normed * jnp.mean(grad * normed, -1, keepdims=True)
    )


def unit_rows(values):
    inverse = lax.rsqrt(jnp.sum(values * values, -1, keepdims=True) + 1e-06)
    return (values * inverse, inverse)


def unit_back(grad, unit, inverse):
    return inverse * (grad - unit * jnp.sum(unit * grad, -1, keepdims=True))


def silu_slope(values):
    sigma = jax.nn.sigmoid(values)
    return sigma * (1.0 + values * (1.0 - sigma))


def inner_product(left, right):
    return lax.dot_general(
        left, right, (((1,), (1,)), ((), ())), preferred_element_type=jnp.float32
    )


def outer_sum(left, right):
    return lax.dot_general(
        left, right, (((0,), (0,)), ((), ())), preferred_element_type=jnp.float32
    )


def causal_mask(scores, q_start):
    rows = q_start + lax.broadcasted_iota(jnp.int32, scores.shape, 0)
    cols = lax.broadcasted_iota(jnp.int32, scores.shape, 1)
    return cols <= rows


def head_forward(query, key, value, q_start, span):
    scale = query.shape[1] ** (-0.5)
    scores = inner_product(query, key) * scale
    weights = jnp.where(causal_mask(scores, q_start), jax.nn.silu(scores) / span, 0.0).astype(
        jnp.bfloat16
    )
    return jnp.dot(weights, value, preferred_element_type=jnp.float32)


def head_backward(query, key, value, d_attn, q_start, span):
    scale = query.shape[1] ** (-0.5)
    scores = inner_product(query, key) * scale
    causal = causal_mask(scores, q_start)
    weights = jnp.where(causal, jax.nn.silu(scores) / span, 0.0).astype(jnp.bfloat16)
    d_weights = inner_product(d_attn, value)
    d_score = jnp.where(causal, d_weights * silu_slope(scores) * (scale / span), 0.0).astype(
        jnp.bfloat16
    )
    d_query = jnp.dot(d_score, key, preferred_element_type=jnp.float32)
    d_key = outer_sum(d_score, query)
    d_value = outer_sum(weights, d_attn)
    return (d_query, d_key, d_value)


def split_heads(values, head_dim):
    return values.reshape(values.shape[0], -1, head_dim).transpose(1, 0, 2)


def join_heads(values):
    return values.transpose(1, 0, 2).reshape(values.shape[1], -1)


def attend(query, key, value, span, head_dim):
    rows = query.shape[0]
    block = min(rows, 512)
    count = rows // block
    q_heads = split_heads(query, head_dim).reshape(-1, count, block, head_dim)
    k_heads = split_heads(key, head_dim)
    v_heads = split_heads(value, head_dim)
    offsets = block * jnp.arange(count, dtype=jnp.int32)

    def one_head(items):
        q_blocks, k_one, v_one = items
        return lax.map(
            lambda pair: head_forward(pair[0], k_one, v_one, pair[1], span), (q_blocks, offsets)
        )

    result = lax.map(one_head, (q_heads, k_heads, v_heads))
    return join_heads(result.reshape(result.shape[0], rows, head_dim))


def attend_back(query, key, value, d_attn, span, head_dim):
    rows = query.shape[0]
    block = min(rows, 512)
    count = rows // block
    q_heads = split_heads(query, head_dim).reshape(-1, count, block, head_dim)
    d_heads = split_heads(d_attn, head_dim).reshape(-1, count, block, head_dim)
    k_heads = split_heads(key, head_dim)
    v_heads = split_heads(value, head_dim)
    offsets = block * jnp.arange(count, dtype=jnp.int32)

    def one_head(items):
        q_blocks, k_one, v_one, d_blocks = items

        def step(carry, piece):
            d_query, d_key, d_value = head_backward(
                piece[0], k_one, v_one, piece[1], piece[2], span
            )
            return ((carry[0] + d_key, carry[1] + d_value), d_query)

        empty = jnp.zeros(k_one.shape, jnp.float32)
        sums, d_query = lax.scan(step, (empty, empty), (q_blocks, d_blocks, offsets))
        return (d_query, sums[0], sums[1])

    d_query, d_key, d_value = lax.map(one_head, (q_heads, k_heads, v_heads, d_heads))
    return (
        join_heads(d_query.reshape(d_query.shape[0], rows, head_dim)),
        join_heads(d_key),
        join_heads(d_value),
    )


def sampled_softmax(
    output, targets, target_ids, valid, normalized_negative_batch, neg_ids, log_item_frequency
):
    normalized_output, y_inv = unit_rows(output)
    normalized_output_batch = normalized_output.astype(jnp.bfloat16)
    normalized_target, t_inv = unit_rows(targets.astype(jnp.float32))
    positive_logits = jnp.sum(normalized_output * normalized_target, -1) / SOFTMAX_TEMP
    negative_logits = (
        inner_product(normalized_output_batch, normalized_negative_batch) / SOFTMAX_TEMP
        - log_item_frequency[None, :]
    )
    keep = target_ids[:, None] != neg_ids[None, :]
    positive_exponent = jnp.exp(positive_logits)
    negative_exponent = jnp.where(keep, jnp.exp(negative_logits), 0.0)
    partition_sum = positive_exponent + jnp.sum(negative_exponent, -1)
    token_weight = valid.astype(jnp.float32)
    loss_sum = jnp.sum(token_weight * (jnp.log(partition_sum) - positive_logits))
    positive_gradient = token_weight * (positive_exponent / partition_sum - 1.0) / SOFTMAX_TEMP
    negative_gradient = (
        negative_exponent * (token_weight / (partition_sum * SOFTMAX_TEMP))[:, None]
    ).astype(jnp.bfloat16)
    d_hat = positive_gradient[:, None] * normalized_target + jnp.dot(
        negative_gradient, normalized_negative_batch, preferred_element_type=jnp.float32
    )
    d_output = unit_back(d_hat, normalized_output, y_inv)
    d_targets = unit_back(positive_gradient[:, None] * normalized_output, normalized_target, t_inv)
    return (loss_sum, normalized_output_batch, negative_gradient, d_output, d_targets)


def local(
    tokens, targets, target_ids, lengths, negatives, negative_ids, negative_counts, w_in, w_out
):
    width = w_out.shape[0]
    head_dim = width // HEADS
    rows = tokens.shape[1]
    span = float(L)
    start = lax.axis_index("hist") * rows
    dp_size = lax.axis_size("dp")
    event_total = float(dp_size * L)
    tok = tokens.reshape(rows, width)
    normed_f, inverse = layer_norm(tok.astype(jnp.float32))
    normed = normed_f.astype(jnp.bfloat16)
    proj = jnp.dot(normed, w_in, preferred_element_type=jnp.float32)
    act = jax.nn.silu(proj).astype(jnp.bfloat16)
    gate_u = act[:, :width]
    value = act[:, width : 2 * width]
    query = act[:, 2 * width : 3 * width]
    key = act[:, 3 * width :]
    n_hat, n_inv = unit_rows(negatives.astype(jnp.float32))
    normalized_negative_batch, neg_ids_all, counts_all = (
        lax.all_gather(n_hat.astype(jnp.bfloat16), "dp", axis=0, tiled=True),
        lax.all_gather(negative_ids, "dp", axis=0, tiled=True),
        lax.all_gather(negative_counts, "dp", axis=0, tiled=True),
    )
    q_group, k_group, v_group = (
        lax.all_to_all(query, "hist", split_axis=1, concat_axis=0, tiled=True),
        lax.all_to_all(key, "hist", split_axis=1, concat_axis=0, tiled=True),
        lax.all_to_all(value, "hist", split_axis=1, concat_axis=0, tiled=True),
    )
    attn_group = attend(q_group, k_group, v_group, span, head_dim).astype(jnp.bfloat16)
    attn = lax.all_to_all(attn_group, "hist", split_axis=0, concat_axis=1, tiled=True)
    attn_normed, attn_inv = layer_norm(attn.astype(jnp.float32))
    gate_f = gate_u.astype(jnp.float32)
    mixed = (attn_normed * gate_f).astype(jnp.bfloat16)
    output = tok.astype(jnp.float32) + jnp.dot(mixed, w_out, preferred_element_type=jnp.float32)
    positions = start + jnp.arange(rows, dtype=jnp.int32)
    valid = positions < lengths[0]
    loss_sum, normalized_output_batch, negative_gradient, d_output, d_targets = sampled_softmax(
        output,
        targets.reshape(rows, width),
        target_ids.reshape(rows),
        valid,
        normalized_negative_batch,
        neg_ids_all,
        jnp.log(counts_all.astype(jnp.float32)),
    )
    d_out_b = d_output.astype(jnp.bfloat16)
    d_mixed = inner_product(d_out_b, w_out)
    d_gate = d_mixed * attn_normed
    d_attn = norm_back(d_mixed * gate_f, attn_normed, attn_inv).astype(jnp.bfloat16)
    d_group = lax.all_to_all(d_attn, "hist", split_axis=1, concat_axis=0, tiled=True)
    group_query, group_key, group_value = attend_back(
        q_group, k_group, v_group, d_group, span, head_dim
    )
    d_query_b, d_key_b, d_value_b = (
        lax.all_to_all(
            group_query.astype(jnp.bfloat16), "hist", split_axis=0, concat_axis=1, tiled=True
        ),
        lax.all_to_all(
            group_key.astype(jnp.bfloat16), "hist", split_axis=0, concat_axis=1, tiled=True
        ),
        lax.all_to_all(
            group_value.astype(jnp.bfloat16), "hist", split_axis=0, concat_axis=1, tiled=True
        ),
    )
    d_act = jnp.concatenate(
        [
            d_gate,
            d_value_b.astype(jnp.float32),
            d_query_b.astype(jnp.float32),
            d_key_b.astype(jnp.float32),
        ],
        1,
    )
    d_proj = (d_act * silu_slope(proj)).astype(jnp.bfloat16)
    d_tokens = (d_output + norm_back(inner_product(d_proj, w_in), normed_f, inverse)).astype(
        jnp.bfloat16
    )
    w_in_part = lax.psum_scatter(outer_sum(normed, d_proj), "dp", scatter_dimension=0, tiled=True)
    w_out_part = lax.psum_scatter(outer_sum(mixed, d_out_b), "dp", scatter_dimension=0, tiled=True)
    neg_part = lax.psum_scatter(
        outer_sum(negative_gradient, normalized_output_batch), "dp", scatter_dimension=0, tiled=True
    )
    w_in_sum, w_out_sum, neg_sum = (
        lax.psum(w_in_part.astype(jnp.bfloat16), "hist").astype(jnp.float32),
        lax.psum(w_out_part.astype(jnp.bfloat16), "hist").astype(jnp.float32),
        lax.psum(neg_part.astype(jnp.bfloat16), "hist").astype(jnp.float32),
    )
    loss = lax.psum(loss_sum, ("dp", "hist")) / event_total
    d_negatives = unit_back(neg_sum, n_hat, n_inv) / event_total
    return (
        loss,
        d_tokens.reshape(1, rows, width),
        d_targets.astype(jnp.bfloat16).reshape(1, rows, width),
        w_in_sum / event_total,
        w_out_sum / event_total,
        d_negatives,
    )


def solution(mesh):
    in_specs = (
        P("dp", "hist", None),
        P("dp", "hist", None),
        P("dp", "hist"),
        P("dp"),
        P("dp", None),
        P("dp"),
        P("dp"),
        P(),
        P(),
    )
    out_specs = (
        P(),
        P("dp", "hist", None),
        P("dp", "hist", None),
        P("dp", None),
        P("dp", None),
        P("dp", None),
    )
    return jax.shard_map(local, mesh=mesh, in_specs=in_specs, out_specs=out_specs, check_vma=False)
```

profile of v0, /device:TPU:1, one launch (start us, length us, event | category | flops | bytes accessed | tf_op | source)
XLA Modules:
  0.0 1563.1 jit_solution(14526671174384913459)
XLA Ops:
  11.9 2.4 multiply_convert_fusion.1
  15.9 6.5 all-to-all-start.2
  23.2 2.8 all-to-all-done.2
  26.0 4.3 all-to-all-start.1
  32.9 305.0 %all-reduce.2 = (s32[2048]{0:T(1024)S(1)}, s32[2048]{0:T(1024)}) all-reduce(s32[2048]{0:T(1024)S(1)} %dynamic-update-slice.1, s32[2048]{0:T(1024)S(1)} %dynamic-update-slice), channel_id=1, replica_groups=mesh['dp'=64,'hist'=4] {'dp'}, use_global_device_ids=true, to_apply=%add.1 | all-reduce | flops 4096 | bytes 32768
  337.9 58.2 %all-to-all-start = ((bf16[128,4,128]{0,2,1:T(8,128)(2,1)}), bf16[128,4,128]{0,2,1:T(8,128)(2,1)S(1)}, u32[]{:S(2)}, u32[]{:S(2)}) async-start(bf16[128,4,128]{0,2,1:T(8,128)(2,1)} %bitcast.13), calls=%async_computation | async-start | bytes 262144 | tf_op jit(solution)/shard_map/all_to_all | solution.py:196
  402.1 4.3 all-to-all-start.3
  406.5 3.5 all-to-all-done.3
  412.1 2.7 fusion.104
  420.1 4.0 fusion.92
  427.4 4.3 all-to-all-start.4
  431.7 4.0 all-to-all-done.4
  436.6 8.0 while.25
  446.3 3.9 all-to-all-start.5
  454.3 3.9 all-to-all-start.6
  459.0 2.9 all-to-all-done.6
  461.9 4.3 all-to-all-start.7
  467.0 3.0 all-to-all-done.7
  471.8 2.8 fusion.93
  474.6 73.2 %psum.28 = f32[]{:T(128)} all-reduce(f32[]{:T(128)} %get-tuple-element.205), channel_id=1, replica_groups=mesh['dp'=64,'hist'=4] {'dp','hist'}, use_global_device_ids=true, to_apply=%region_12.13 | all-reduce | flops 1 | bytes 8 | tf_op jit(solution)/shard_map/psum | solution.py:259
  549.5 175.6 %reduce-scatter.6.cloned.1.call-done = f32[8,512]{1,0:T(8,128)} async-done(((f32[512,512]{1,0:T(8,128)}), f32[8,512]{1,0:T(8,128)}) %reduce-scatter.6.cloned.1.call-update) | async-done | bytes 16400 | tf_op jit(solution)/shard_map/reduce_scatter | solution.py:250
  726.4 366.5 %reduce-scatter.8.cloned.1.call-done = f32[32,512]{1,0:T(8,128)} async-done(((f32[2048,512]{1,0:T(8,128)}), f32[32,512]{1,0:T(8,128)}) %reduce-scatter.8.cloned.1.call-update) | async-done | bytes 65552 | tf_op jit(solution)/shard_map/reduce_scatter | solution.py:251
  1094.3 366.9 %reduce-scatter.4.cloned.1.call-done = f32[8,2048]{1,0:T(8,128)} async-done(((f32[512,2048]{1,0:T(8,128)}), f32[8,2048]{1,0:T(8,128)}) %reduce-scatter.4.cloned.1.call-update) | async-done | bytes 65552 | tf_op jit(solution)/shard_map/reduce_scatter | solution.py:249
  1463.5 86.8 %all-reduce.6.cloned.1.call-done = (bf16[8,2048]{1,0:T(8,128)(2,1)}, bf16[8,512]{1,0:T(8,128)(2,1)}, bf16[32,512]{1,0:T(8,128)(2,1)}) async-done(((bf16[8,2048]{1,0:T(8,128)(2,1)}, bf16[8,512]{1,0:T(8,128)(2,1)}, bf16[32,512]{1,0:T(8,128)(2,1)}), (bf16[8,2048]{1,0:T(8,128)(2,1)}, bf16[8,512]{1,0:T(8,128)(2,1)}, bf16[32,512]{1,0:T(8,128)(2,1)})) %all-reduce.6.cloned.1.call-update) | async-done | bytes 73744 | tf_op jit(solution)/shard_map/psum | solution.py:255
  (157 shorter events, 54.8 us)
Async XLA Ops:
  7.2 404.9 %all-gather.2.cloned.1.call-start = ((), (), s32[]{:S(2)}) async-start(), calls=%async_computation.11 | async-start | bytes 2129920 | tf_op jit(solution)/shard_map/all_gather | solution.py:191
  14.3 16.8 %copy-start.24 = (u32[256]{0:T(256)S(1)}, u32[256]{0:T(256)}, u32[]{:S(2)}) copy-start(u32[256]{0:T(256)} %constant.141) | copy-start | bytes 3076
  14.3 18.1 %copy-start.21 = (s32[32]{0:T(128)S(1)}, s32[32]{0:T(128)}, u32[]{:S(2)}) copy-start(s32[32]{0:T(128)} %param.19) | copy-start | bytes 388
  14.3 18.3 %copy-start.22 = (s32[32]{0:T(128)S(1)}, s32[32]{0:T(128)}, u32[]{:S(2)}) copy-start(s32[32]{0:T(128)} %param.18) | copy-start | bytes 388
  15.9 10.1 all-to-all-start.2
  26.0 311.9 %all-to-all-start.1 = ((bf16[128,4,128]{0,2,1:T(8,128)(2,1)}), bf16[128,4,128]{0,2,1:T(8,128)(2,1)S(1)}, u32[]{:S(2)}, u32[]{:S(2)}) async-start(bf16[128,4,128]{0,2,1:T(8,128)(2,1)} %bitcast.17), calls=%async_computation.1 | async-start | bytes 262144 | tf_op jit(solution)/shard_map/all_to_all | solution.py:197
  337.9 61.8 %all-to-all-start = ((bf16[128,4,128]{0,2,1:T(8,128)(2,1)}), bf16[128,4,128]{0,2,1:T(8,128)(2,1)S(1)}, u32[]{:S(2)}, u32[]{:S(2)}) async-start(bf16[128,4,128]{0,2,1:T(8,128)(2,1)} %bitcast.13), calls=%async_computation | async-start | bytes 262144 | tf_op jit(solution)/shard_map/all_to_all | solution.py:196
  400.1 10.3 copy-start.1
  401.2 9.1 copy-start.7
  401.2 10.9 copy-start.12
  401.2 10.9 copy-start.20
  401.2 10.9 copy-start.23
  402.1 7.9 all-to-all-start.3
  406.4 318.6 %reduce-scatter.6.cloned.1.call-start = ((), (), s32[]{:S(2)}) async-start(), calls=%async_computation.13 | async-start | bytes 1064960 | tf_op jit(solution)/shard_map/reduce_scatter | solution.py:250
  420.0 672.9 %reduce-scatter.8.cloned.1.call-start = ((), (), s32[]{:S(2)}) async-start(), calls=%async_computation.14 | async-start | bytes 4259840 | tf_op jit(solution)/shard_map/reduce_scatter | solution.py:251
  427.4 8.4 all-to-all-start.4
  446.3 8.0 all-to-all-start.5
  454.3 7.6 all-to-all-start.6
  458.2 13.5 copy-start.17
  461.9 8.0 all-to-all-start.7
  466.2 995.0 %reduce-scatter.4.cloned.1.call-start = ((), (), s32[]{:S(2)}) async-start(), calls=%async_computation.12 | async-start | bytes 4259840 | tf_op jit(solution)/shard_map/reduce_scatter | solution.py:249
  474.6 1075.7 %copy-start.6 = (bf16[32,512]{1,0:T(8,128)(2,1)S(1)}, bf16[32,512]{1,0:T(8,128)(2,1)}, u32[]{:S(2)}) copy-start(bf16[32,512]{1,0:T(8,128)(2,1)} %param.17) | copy-start | bytes 98308
  474.6 1075.7 %copy-start.15 = (f32[32]{0:T(128)S(1)}, f32[32]{0:T(128)}, u32[]{:S(2)}) copy-start(f32[32]{0:T(128)} %copy-done.14) | copy-start | bytes 388
  474.6 1075.7 %all-reduce.6.cloned.1.call-start = ((), (), s32[]{:S(2)}) async-start(), calls=%async_computation.15 | async-start | bytes 147456 | tf_op jit(solution)/shard_map/psum | solution.py:255
  (18 other events, 44.5 us)
Sparse Core Ops, SparseCore 0:
  12.2 118.2 all-gather.1
  420.1 304.8 reduce-scatter.5
  727.7 365.0 reduce-scatter.7
  1095.2 365.9 reduce-scatter.3
  1464.7 85.5 all-reduce.5
where the time goes:
time: 1560 us
  waiting for transfers between devices  1020 us (65%)
  blocking collectives  378 us (24%)
  starting transfers between devices  90 us (6%)
  matrix products  26 us (2%)
  other arithmetic  22.5 us (1%)
  between operations  17.3 us (1%)
    reduce_scatter x1, waiting for transfers between devices, local(): lax.psum_scatter(outer_sum(normed, d_proj), 'dp', scatter_dimension=0, ti...  367 us
    reduce_scatter x1, waiting for transfers between devices, local(): lax.psum_scatter(outer_sum(negative_gradient, normalized_output_batch), '...  366 us
    unnamed x1, blocking collectives  305 us
    reduce_scatter x1, waiting for transfers between devices, local(): lax.psum_scatter(outer_sum(mixed, d_out_b), 'dp', scatter_dimension=0, ti...  176 us
    psum x1, waiting for transfers between devices, local(): lax.psum(w_in_part.astype(jnp.bfloat16), 'hist').astype(jnp.float32)  86.8 us
    psum x1, blocking collectives, local(): loss = lax.psum(loss_sum, ('dp', 'hist')) / event_total  73.2 us
    all_to_all x1, starting transfers between devices, local(): lax.all_to_all(query, 'hist', split_axis=1, concat_axis=0, tiled=True)  58.2 us
  transfers between devices with their start and end apart: 13, of which 11 were waited for; matrix products, arithmetic and copies ran while one was open for 3% of the time, Pallas kernels for 0%

commit v1 on v0

v1 whole, which is shorter than its diff:
```python
import functools

import jax
import jax.numpy as jnp
from jax import lax
from jax.experimental import pallas as pl
from jax.experimental.pallas import tpu as pltpu
from jax.sharding import PartitionSpec as P

HEADS = 8
L = 512
W = 512
HIST = 4
R = 128
NB = 32
NQ = NB // HIST
TEMP = 0.05
MESH = pl.DeviceIdType.MESH
F32 = jnp.float32
BF16 = jnp.bfloat16


def layer_norm(values):
    centered = values - jnp.mean(values, -1, keepdims=True)
    inverse = lax.rsqrt(jnp.mean(centered * centered, -1, keepdims=True) + 1e-06)
    return (centered * inverse, inverse)


def norm_back(grad, normed, inverse):
    return inverse * (
        grad
        - jnp.mean(grad, -1, keepdims=True)
        - normed * jnp.mean(grad * normed, -1, keepdims=True)
    )


def unit_rows(values):
    inverse = lax.rsqrt(jnp.sum(values * values, -1, keepdims=True) + 1e-06)
    return (values * inverse, inverse)


def unit_back(grad, unit, inverse):
    return inverse * (grad - unit * jnp.sum(unit * grad, -1, keepdims=True))


def sigmoid(values):
    return 0.5 * jnp.tanh(0.5 * values) + 0.5


def silu_slope(values):
    sigma = sigmoid(values)
    return sigma * (1.0 + values * (1.0 - sigma))


def silu(values):
    return values * sigmoid(values)


def inner_product(left, right):
    return lax.dot_general(left, right, (((1,), (1,)), ((), ())), preferred_element_type=F32)


def matmul(left, right):
    return jnp.dot(left, right, preferred_element_type=F32)


def plan(mesh):
    dp = mesh.shape["dp"]
    if dp == 64:
        return 8, 2, 4
    return 2, 1, dp // 2


def kernel(
    sizes,
    count,
    tok_ref,
    tgt_ref,
    tid_ref,
    len_ref,
    neg_ref,
    nid_ref,
    ncnt_ref,
    win_ref,
    wout_ref,
    loss_ref,
    dtok_ref,
    dtgt_ref,
    dwin_ref,
    dwout_ref,
    dneg_ref,
    tok_all,
    nrm_all,
    nrmf,
    proj,
    gate,
    k_all,
    v_all,
    q_all,
    slope,
    attn,
    nall,
    idz,
    idp,
    idb,
    lcb,
    ex,
    ngo,
    ngs,
    nga,
    my_all,
    da_all,
    dps,
    dpa,
    dpo,
    dout,
    rsa_s,
    rsa_r,
    za_s,
    za_r,
    ea,
    rsb_s,
    rsb_r,
    zb_s,
    zb_r,
    eb,
    l1,
    l2,
    l3,
    ssem,
    rsem,
):
    nz, nyh, nx = sizes
    npl = nyh * nx
    dp_size = nz * npl
    rw = W // dp_size
    total_events = float(dp_size * L)
    d = lax.axis_index("dp")
    h = lax.axis_index("hist")
    z = lax.div(d, npl)
    p = lax.rem(d, npl)
    yh = lax.div(p, nx)
    x = lax.rem(p, nx)
    core = lax.rem(h, 2)
    sib = h + 1 - 2 * core

    def hist_to(o):
        return lax.rem(h + o, HIST)

    def hist_from(o):
        return lax.rem(h + HIST - o, HIST)

    def z_to(o):
        return lax.rem(z + o, nz)

    def z_from(o):
        return lax.rem(z + nz - o, nz)

    offsets = [(a, b) for a in range(nyh) for b in range(nx) if (a, b) != (0, 0)]

    def p_to(ab):
        return lax.rem(yh + ab[0], nyh) * nx + lax.rem(x + ab[1], nx)

    def p_from(ab):
        return lax.rem(yh + nyh - ab[0], nyh) * nx + lax.rem(x + nx - ab[1], nx)

    def hist_dev(index):
        return {"dp": d, "hist": index}

    def z_dev(index):
        return {"dp": index * npl + p, "hist": h}

    def p_dev(index):
        return {"dp": z * npl + index, "hist": h}

    sends = []
    taken = [0]

    def slots(number):
        base = taken[0]
        taken[0] += number
        assert taken[0] <= count
        return base

    def send(src, dst, slot, device):
        copy = pltpu.make_async_remote_copy(
            src_ref=src,
            dst_ref=dst,
            send_sem=ssem.at[slot],
            recv_sem=rsem.at[slot],
            device_id=device,
            device_id_type=MESH,
        )
        copy.start()
        sends.append(copy)

    def recv(dst, slot):
        pltpu.make_async_remote_copy(
            src_ref=dst,
            dst_ref=dst,
            send_sem=ssem.at[slot],
            recv_sem=rsem.at[slot],
            device_id=hist_dev(sib),
            device_id_type=MESH,
        ).wait_recv()

    barrier = pltpu.get_barrier_semaphore()
    peers = (
        [hist_dev(hist_to(o)) for o in range(1, HIST)]
        + [p_dev(p_to(ab)) for ab in offsets]
        + [z_dev(z_to(o)) for o in range(1, nz)]
    )
    for device in peers:
        pl.semaphore_signal(barrier, inc=1, device_id=device, device_id_type=MESH)

    n_hat, n_inv = unit_rows(neg_ref[...].astype(F32))
    n_hat_b = n_hat.astype(BF16)
    nall[core, p, z] = jnp.where(core == 0, n_hat_b[:, :256], n_hat_b[:, 256:])
    row_at = lax.broadcasted_iota(jnp.int32, (8, 128), 0)
    lane_at = lax.broadcasted_iota(jnp.int32, (8, 128), 1)
    own_place = (row_at == z) & (lane_at >= x * NB) & (lane_at < x * NB + NB)
    for kind, ref in enumerate((nid_ref, ncnt_ref)):
        wide = jnp.concatenate([ref[...]] * (128 // NB), axis=1)
        idz[z, kind * 8 : kind * 8 + 8] = jnp.where(own_place, wide, 0)

    pl.semaphore_wait(barrier, len(peers))

    s_tok = slots(HIST)
    for o in range(1, HIST):
        send(tok_ref, tok_all.at[h], s_tok + o, hist_dev(hist_to(o)))
    s_nz = slots(nz)
    s_iz = slots(nz)
    for o in range(1, nz):
        send(nall.at[core, p, z], nall.at[core, p, z], s_nz + o, z_dev(z_to(o)))
        send(idz.at[z], idz.at[z], s_iz + o, z_dev(z_to(o)))

    tokf = tok_ref[...].astype(F32)
    normed_f, inverse = layer_norm(tokf)
    nrmf[...] = normed_f
    normed = normed_f.astype(BF16)
    nrm_all[h] = normed
    for blk, ref in enumerate((gate, v_all.at[h], q_all.at[h], k_all.at[h])):
        cols = slice(blk * W, (blk + 1) * W)
        part = matmul(normed, win_ref[:, cols])
        proj[:, cols] = part
        ref[...] = silu(part).astype(BF16)

    for o in range(1, nz):
        recv(nall.at[core, p, z_from(o)], s_nz + o)
        recv(idz.at[z_from(o)], s_iz + o)
    tile = idz[0]
    for k in range(1, nz):
        tile = tile + idz[k]
    idp[p] = tile
    s_np = slots(npl)
    s_ip = slots(npl)
    for k, ab in enumerate(offsets):
        send(nall.at[core, p], nall.at[core, p], s_np + k, p_dev(p_to(ab)))
        send(idp.at[p], idp.at[p], s_ip + k, p_dev(p_to(ab)))
    s_sib = slots(npl)
    send(nall.at[core, p], nall.at[core, p], s_sib + npl - 1, hist_dev(sib))

    for o in range(1, HIST):
        b = hist_from(o)
        recv(tok_all.at[b], s_tok + o)
        other = layer_norm(tok_all[b].astype(F32))[0].astype(BF16)
        nrm_all[b] = other
        v_all[b] = silu(matmul(other, win_ref[:, W : 2 * W])).astype(BF16)
        k_all[b] = silu(matmul(other, win_ref[:, 3 * W :])).astype(BF16)

    lane = lax.broadcasted_iota(jnp.int32, (1, 128), 1)
    low = lane < 64
    half_mask = [jnp.where(low, 1.0, 0.0).astype(BF16), jnp.where(low, 0.0, 1.0).astype(BF16)]
    causal = lax.broadcasted_iota(jnp.int32, (R, L), 1) <= h * R + lax.broadcasted_iota(
        jnp.int32, (R, L), 0
    )
    scale = 0.125

    def forward_pair(n, carry):
        cols = pl.ds(pl.multiple_of(n * 128, 128), 128)
        q = q_all[h, :, cols]
        k = k_all[:, :, cols].reshape(L, 128)
        v = v_all[:, :, cols].reshape(L, 128)
        halves = []
        for e in range(2):
            s = inner_product(q * half_mask[e], k) * scale
            sigma = sigmoid(s)
            w = jnp.where(causal, s * sigma * (1.0 / L), 0.0).astype(BF16)
            slope[2 * n + e] = jnp.where(
                causal, sigma * (1.0 + s * (1.0 - sigma)) * (scale / L), 0.0
            )
            halves.append(matmul(w, v))
        attn[:, cols] = jnp.where(low, halves[0], halves[1]).astype(BF16)
        return carry

    lax.fori_loop(0, HEADS // 2, forward_pair, 0)

    attn_normed, attn_inv = layer_norm(attn[...].astype(F32))
    gate_f = gate[...].astype(F32)
    mixed = (attn_normed * gate_f).astype(BF16)
    my_all[h, :, :W] = mixed
    output = tok_ref[...].astype(F32) + matmul(mixed, wout_ref[...])
    y_hat, y_inv = unit_rows(output)
    y_hat_b = y_hat.astype(BF16)
    my_all[h, :, W:] = y_hat_b
    s_my = slots(HIST)
    for o in range(1, HIST):
        send(my_all.at[h], my_all.at[h], s_my + o, hist_dev(hist_to(o)))
    t_hat, t_inv = unit_rows(tgt_ref[...].astype(F32))
    pos_col = jnp.sum(y_hat * t_hat, -1, keepdims=True) / TEMP
    pos_row = jnp.broadcast_to(pos_col, (R, 128)).T[0:1, :]

    for k, ab in enumerate(offsets):
        src = p_from(ab)
        recv(nall.at[core, src], s_np + k)
        recv(idp.at[src], s_ip + k)
        send(nall.at[core, src], nall.at[core, src], s_sib + k, hist_dev(sib))
    for a in range(nyh):
        both = idp[a * nx]
        for b in range(1, nx):
            both = both + idp[a * nx + b]
        ids = both[:8].astype(F32)
        logs = jnp.log(jnp.maximum(both[8:].astype(F32), 1.0))
        turned = jnp.concatenate([ids, logs, jnp.zeros((112, 128), F32)], axis=0).T
        for b in range(nx):
            rows = turned[b * NB : (b + 1) * NB]
            for k in range(nz):
                at = pl.ds(k * NB, NB)
                idb[a * nx + b, at] = jnp.broadcast_to(rows[:, k : k + 1], (NB, 128))
                lcb[a * nx + b, at] = jnp.broadcast_to(rows[:, 8 + k : 9 + k], (NB, 128))
    other_core = 1 - core
    recv(nall.at[other_core, p], s_sib + npl - 1)
    for k, ab in enumerate(offsets):
        recv(nall.at[other_core, p_from(ab)], s_sib + k)

    tid_row = tid_ref[...].astype(F32)

    def logits_chunk(c, acc):
        lg = inner_product(nall[0, c].reshape(nz * NB, 256), y_hat_b[:, :256]) + inner_product(
            nall[1, c].reshape(nz * NB, 256), y_hat_b[:, 256:]
        )
        lg = lg * (1.0 / TEMP) - lcb[c]
        value = jnp.where(idb[c] != tid_row, jnp.exp(lg), 0.0)
        ex[c] = value
        return acc + jnp.sum(value.reshape(nz * NB // 8, 8, 128), 0)

    acc = lax.fori_loop(0, npl, logits_chunk, jnp.zeros((8, 128), F32))
    total = jnp.exp(pos_row) + jnp.sum(acc, 0, keepdims=True)
    position = h * R + lax.broadcasted_iota(jnp.int32, (1, 128), 1)
    valid = jnp.where(position < len_ref[...], 1.0, 0.0)
    loss = jnp.sum(valid * (jnp.log(total) - pos_row), -1, keepdims=True)
    l1[p] = jnp.broadcast_to(loss, (8, 128))
    s_l1 = slots(npl)
    for k, ab in enumerate(offsets):
        send(l1.at[p], l1.at[p], s_l1 + k, p_dev(p_to(ab)))
    pg_row = valid * (jnp.exp(pos_row) / total - 1.0) / TEMP
    pg = jnp.broadcast_to(pg_row, (128, 128)).T[:, 0:1]
    scale_row = valid / (total * TEMP)

    def grad_chunk(c, carry):
        g = ex[c] * scale_row
        ngo[c] = g.astype(BF16)
        g4 = g.reshape(nz, HIST, NQ, 128)
        for q in range(HIST):
            ngs[q, c] = g4[:, q].reshape(nz * NQ, 128).astype(BF16)
        return carry

    lax.fori_loop(0, npl, grad_chunk, 0)
    ng = ngo[...].reshape(dp_size * NB, 128).T
    d_hat = pg * t_hat + jnp.concatenate(
        [matmul(ng, nall[c].reshape(dp_size * NB, 256)) for c in range(2)], axis=1
    )
    d_out = unit_back(d_hat, y_hat, y_inv)
    dout[...] = d_out
    dtgt_ref[...] = unit_back(pg * y_hat, t_hat, t_inv).astype(BF16)
    d_out_b = d_out.astype(BF16)
    d_mixed = inner_product(d_out_b, wout_ref[...])
    da_all[h] = norm_back(d_mixed * gate_f, attn_normed, attn_inv).astype(BF16)
    s_da = slots(HIST)
    for o in range(1, HIST):
        send(da_all.at[h], da_all.at[h], s_da + o, hist_dev(hist_to(o)))
    d_gate = (d_mixed * attn_normed * silu_slope(proj[:, :W])).astype(BF16)
    dpo[:, :W] = d_gate
    for n in range(HIST):
        cols = slice(n * 128, (n + 1) * 128)
        dps[n, :, 0:128] = d_out_b[:, cols]
        dps[n, :, 128:256] = d_gate[:, cols]
    s_dg = slots(HIST)
    s_ng = slots(HIST)
    for o in range(1, HIST):
        to = hist_to(o)
        send(dps.at[to, :, pl.ds(0, 256)], dpa.at[h, :, pl.ds(0, 256)], s_dg + o, hist_dev(to))
    for o in range(1, HIST):
        to = hist_to(o)
        send(ngs.at[to], nga.at[h], s_ng + o, hist_dev(to))
    nga[h] = ngs[h]

    for k, ab in enumerate(offsets):
        recv(l1.at[p_from(ab)], s_l1 + k)
    part = l1[0]
    for k in range(1, npl):
        part = part + l1[k]
    l2[z] = part
    s_l2 = slots(nz)
    for o in range(1, nz):
        send(l2.at[z], l2.at[z], s_l2 + o, z_dev(z_to(o)))

    def query_pair(n, carry):
        cols = pl.ds(pl.multiple_of(n * 128, 128), 128)
        da = da_all[h, :, cols]
        k = k_all[:, :, cols].reshape(L, 128)
        v = v_all[:, :, cols].reshape(L, 128)
        halves = []
        for e in range(2):
            dw = inner_product(da * half_mask[e], v)
            halves.append(matmul((dw * slope[2 * n + e]).astype(BF16), k))
        dq = jnp.where(low, halves[0], halves[1]).astype(BF16).astype(F32)
        at = pl.ds(pl.multiple_of(2 * W + n * 128, 128), 128)
        piece = (dq * silu_slope(proj[:, at])).astype(BF16)
        dpo[:, at] = piece
        dps[n, :, 384:512] = piece
        return carry

    lax.fori_loop(0, HEADS // 2, query_pair, 0)
    for o in range(1, HIST):
        b = hist_from(o)
        q_all[b] = silu(matmul(nrm_all[b], win_ref[:, 2 * W : 3 * W])).astype(BF16)
    for o in range(1, HIST):
        recv(da_all.at[hist_from(o)], s_da + o)

    causal_t = lax.broadcasted_iota(jnp.int32, (R, L), 1) >= h * R + lax.broadcasted_iota(
        jnp.int32, (R, L), 0
    )

    def key_pair(n):
        cols = pl.ds(pl.multiple_of(n * 128, 128), 128)
        k = k_all[h, :, cols]
        v = v_all[h, :, cols]
        q = q_all[:, :, cols].reshape(L, 128)
        da = da_all[:, :, cols].reshape(L, 128)
        dks, dvs = [], []
        for e in range(2):
            s = inner_product(k * half_mask[e], q) * scale
            sigma = sigmoid(s)
            w = jnp.where(causal_t, s * sigma * (1.0 / L), 0.0).astype(BF16)
            dw = inner_product(v * half_mask[e], da)
            ds = jnp.where(
                causal_t, dw * (sigma * (1.0 + s * (1.0 - sigma))) * (scale / L), 0.0
            ).astype(BF16)
            dks.append(matmul(ds, q))
            dvs.append(matmul(w, da))
        for at, parts, place in ((W, dvs, 256), (3 * W, dks, 512)):
            grad = jnp.where(low, parts[0], parts[1]).astype(BF16).astype(F32)
            at = pl.ds(pl.multiple_of(at + n * 128, 128), 128)
            piece = (grad * silu_slope(proj[:, at])).astype(BF16)
            dpo[:, at] = piece
            dps[n, :, place : place + 128] = piece

    s_dp = slots(HIST)
    for o in range(1, HIST + 1):
        n = hist_to(o)
        key_pair(n)
        if o < HIST:
            send(dps.at[n, :, pl.ds(256, 384)], dpa.at[h, :, pl.ds(256, 384)], s_dp + o, hist_dev(n))
    dpa[h] = dps[h]

    for o in range(1, HIST):
        recv(my_all.at[hist_from(o)], s_my + o)
        recv(nga.at[hist_from(o)], s_ng + o)

    def neg_chunk(c, carry):
        left = jnp.concatenate([nga[k, c] for k in range(HIST)], axis=1)
        rsa_s[c] = matmul(left, my_all[:, :, W:].reshape(L, W)).astype(BF16)
        return carry

    lax.fori_loop(0, npl, neg_chunk, 0)
    s_ra = slots(npl)
    for k, ab in enumerate(offsets):
        to = p_to(ab)
        send(rsa_s.at[to], rsa_r.at[k], s_ra + k, p_dev(to))

    for o in range(1, HIST):
        recv(dpa.at[hist_from(o), :, pl.ds(0, 256)], s_dg + o)
        recv(dpa.at[hist_from(o), :, pl.ds(256, 384)], s_dp + o)

    def spread(result, c0, width):
        parts = result.reshape(nz, npl, rw, width)
        for c in range(npl):
            rsb_s[c, :, c0 : c0 + width] = parts[:, c].reshape(nz * rw, width).astype(BF16)

    mixed_t = my_all[:, :, :W].reshape(L, W).T
    spread(matmul(mixed_t, dpa[:, :, 0:128].reshape(L, 128)), 0, 128)
    normed_t = nrm_all[...].reshape(L, W).T
    for c0 in (128, 384):
        spread(matmul(normed_t, dpa[:, :, c0 : c0 + 256].reshape(L, 256)), c0, 256)
    s_rb = slots(npl)
    for k, ab in enumerate(offsets):
        to = p_to(ab)
        send(rsb_s.at[to], rsb_r.at[k], s_rb + k, p_dev(to))

    for o in range(1, nz):
        recv(l2.at[z_from(o)], s_l2 + o)
    part = l2[0]
    for k in range(1, nz):
        part = part + l2[k]
    l3[h] = part
    s_l3 = slots(HIST)
    for o in range(1, HIST):
        send(l3.at[h], l3.at[h], s_l3 + o, hist_dev(hist_to(o)))

    grad = inner_product(dpo[...], win_ref[...])
    dtok_ref[...] = (dout[...] + norm_back(grad, nrmf[...], inverse)).astype(BF16)

    def over_plane(src, arrived, base, out):
        total = src[p].astype(F32)
        for k in range(len(offsets)):
            recv(arrived.at[k], base + k)
            total = total + arrived[k].astype(F32)
        out[...] = total.reshape(out.shape)
        slot = slots(nz)
        return slot

    def over_z(out, arrived, slot):
        for o in range(1, nz):
            to = z_to(o)
            send(out.at[to], arrived.at[o], slot + o, z_dev(to))

    def sum_z(out, arrived, slot):
        total = out[z]
        for o in range(1, nz):
            recv(arrived.at[o], slot + o)
            total = total + arrived[o]
        return total

    s_za = over_plane(rsa_s, rsa_r, s_ra, za_s)
    over_z(za_s, za_r, s_za)
    s_zb = over_plane(rsb_s, rsb_r, s_rb, zb_s)
    over_z(zb_s, zb_r, s_zb)
    s_ea = slots(HIST)
    s_eb = slots(HIST)
    ea[h] = sum_z(za_s, za_r, s_za)
    for o in range(1, HIST):
        send(ea.at[h], ea.at[h], s_ea + o, hist_dev(hist_to(o)))
    eb[h] = sum_z(zb_s, zb_r, s_zb)
    for o in range(1, HIST):
        send(eb.at[h], eb.at[h], s_eb + o, hist_dev(hist_to(o)))

    for o in range(1, HIST):
        recv(l3.at[hist_from(o)], s_l3 + o)
    part = l3[0]
    for k in range(1, HIST):
        part = part + l3[k]
    loss_ref[...] = part / total_events
    for o in range(1, HIST):
        recv(ea.at[hist_from(o)], s_ea + o)
    d_nhat = ea[...].reshape(NB, W)
    dneg_ref[...] = unit_back(d_nhat, n_hat, n_inv) / total_events
    for o in range(1, HIST):
        recv(eb.at[hist_from(o)], s_eb + o)
    for k in range(HIST):
        dwout_ref[:, k * 128 : (k + 1) * 128] = eb[k, :, 0:128] / total_events
        for blk in range(4):
            dwin_ref[:, blk * W + k * 128 : blk * W + (k + 1) * 128] = (
                eb[k, :, (blk + 1) * 128 : (blk + 2) * 128] / total_events
            )
    for copy in sends:
        copy.wait_send()


def local(sizes, *args):
    tokens, targets, target_ids, lengths, negatives, negative_ids, counts, w_in, w_out = args
    nz, nyh, nx = sizes
    npl = nyh * nx
    dp_size = nz * npl
    rw = W // dp_size
    vmem = pltpu.VMEM
    count = 256
    scratch = [
        vmem((HIST, R, W), BF16),
        vmem((HIST, R, W), BF16),
        vmem((R, W), F32),
        vmem((R, 4 * W), F32),
        vmem((R, W), BF16),
        vmem((HIST, R, W), BF16),
        vmem((HIST, R, W), BF16),
        vmem((HIST, R, W), BF16),
        vmem((HEADS, R, L), F32),
        vmem((R, W), BF16),
        vmem((2, npl, nz, NB, 256), BF16),
        vmem((nz, 16, 128), jnp.int32),
        vmem((npl, 16, 128), jnp.int32),
        vmem((npl, nz * NB, 128), F32),
        vmem((npl, nz * NB, 128), F32),
        vmem((npl, nz * NB, 128), F32),
        vmem((npl, nz * NB, 128), BF16),
        vmem((HIST, npl, nz * NQ, 128), BF16),
        vmem((HIST, npl, nz * NQ, 128), BF16),
        vmem((HIST, R, 2 * W), BF16),
        vmem((HIST, R, W), BF16),
        vmem((HIST, R, 640), BF16),
        vmem((HIST, R, 640), BF16),
        vmem((R, 4 * W), BF16),
        vmem((R, W), F32),
        vmem((npl, nz * NQ, W), BF16),
        vmem((npl, nz * NQ, W), BF16),
        vmem((nz, NQ, W), F32),
        vmem((nz, NQ, W), F32),
        vmem((HIST, NQ, W), F32),
        vmem((npl, nz * rw, 640), BF16),
        vmem((npl, nz * rw, 640), BF16),
        vmem((nz, rw, 640), F32),
        vmem((nz, rw, 640), F32),
        vmem((HIST, rw, 640), F32),
        vmem((npl, 8, 128), F32),
        vmem((nz, 8, 128), F32),
        vmem((HIST, 8, 128), F32),
        pltpu.SemaphoreType.DMA((count,)),
        pltpu.SemaphoreType.DMA((count,)),
    ]
    shape = jax.ShapeDtypeStruct
    outs = pl.pallas_call(
        functools.partial(kernel, sizes, count),
        out_shape=[
            shape((8, 128), F32),
            shape((R, W), BF16),
            shape((R, W), BF16),
            shape((rw, 4 * W), F32),
            shape((rw, W), F32),
            shape((NB, W), F32),
        ],
        in_specs=[pl.BlockSpec(memory_space=pltpu.VMEM)] * 9,
        out_specs=[pl.BlockSpec(memory_space=pltpu.VMEM)] * 6,
        scratch_shapes=scratch,
        compiler_params=pltpu.CompilerParams(
            collective_id=0, has_side_effects=True, vmem_limit_bytes=48 * 1024 * 1024
        ),
    )(
        tokens.reshape(R, W),
        targets.reshape(R, W),
        target_ids,
        lengths.reshape(1, 1),
        negatives,
        negative_ids.reshape(1, NB),
        counts.reshape(1, NB),
        w_in,
        w_out,
    )
    return (
        outs[0][0, 0],
        outs[1].reshape(1, R, W),
        outs[2].reshape(1, R, W),
        outs[3],
        outs[4],
        outs[5],
    )


def solution(mesh):
    in_specs = (
        P("dp", "hist", None),
        P("dp", "hist", None),
        P("dp", "hist"),
        P("dp"),
        P("dp", None),
        P("dp"),
        P("dp"),
        P(),
        P(),
    )
    out_specs = (
        P(),
        P("dp", "hist", None),
        P("dp", "hist", None),
        P("dp", None),
        P("dp", None),
        P("dp", None),
    )
    return jax.shard_map(
        functools.partial(local, plan(mesh)),
        mesh=mesh,
        in_specs=in_specs,
        out_specs=out_specs,
        check_vma=False,
    )
```

time: 1560 us -> 100 us (0.06)
  waiting for transfers between devices: 1020 us -> 0 us
  blocking collectives: 378 us -> 0 us
  starting transfers between devices: 90 us -> 0 us
  Pallas kernels: 0 us -> 87.6 us
  matrix products: 26 us -> 0 us
  other arithmetic: 22.5 us -> 0 us
  between operations: 17.3 us -> 1.31 us
    reduce_scatter x3 -> x0, waiting for transfers between devices: 909 us -> none  [the longest x1 367 us: local(): lax.psum_scatter(outer_sum(normed, d_proj), 'dp', scatter_dimension=0, ti...]
    unnamed x1 -> x0, blocking collectives: 305 us -> none
    all_to_all x8 -> x0, starting transfers between devices: 89.9 us -> none  [the longest x1 58.2 us: local(): lax.all_to_all(query, 'hist', split_axis=1, concat_axis=0, tiled=True)]
    pallas_call x0 -> x1, Pallas kernels: none -> 87.6 us  [local(): pl.pallas_call(functools.partial(kernel, sizes, count), out_shape=[shape(...]
    psum x1 -> x0, waiting for transfers between devices: 86.8 us -> none  [local(): lax.psum(w_in_part.astype(jnp.bfloat16), 'hist').astype(jnp.float32)]
    psum x1 -> x0, blocking collectives: 73.2 us -> none  [local(): loss = lax.psum(loss_sum, ('dp', 'hist')) / event_total]
    dot_general x21 -> x0, matrix products: 26 us -> none  [the longest x7 13.3 us: outer_sum(): lax.dot_general(left, right, (((0,), (0,)), ((), ())), preferred_element_...]
    all_to_all x8 -> x0, waiting for transfers between devices: 19.4 us -> none  [the longest x1 4.02 us: local(): lax.all_to_all(d_attn, 'hist', split_axis=1, concat_axis=0, tiled=True)]
  transfers between devices with their start and end apart: 13 -> 0, of which waited for: 11 -> 0; matrix products, arithmetic and copies ran while one was open for 3% -> 0% of each run, Pallas kernels for 0% -> 0%
where the time goes in v1:
time: 100 us; the launch traced here: 99.7 us
  Pallas kernels  87.6 us (88%)
  local copies, waits for them, and re-layouts  10.8 us (11%)
  between operations  1.31 us (1%)
    pallas_call x1, Pallas kernels, local(): pl.pallas_call(functools.partial(kernel, sizes, count), out_shape=[shape(...  87.6 us
    unnamed x21, local copies, waits for them, and re-layouts  10.3 us

profile of v1, /device:TPU:1, one launch (start us, length us, event | category | flops | bytes accessed | tf_op | source)
XLA Modules:
  0.0 99.7 jit_solution(6220518063846307567)
XLA Ops:
  1.3 0.0 copy-start
  1.3 1.6 %copy-done = bf16[512,2048]{1,0:T(8,128)(2,1)S(1)} copy-done((bf16[512,2048]{1,0:T(8,128)(2,1)S(1)}, bf16[512,2048]{1,0:T(8,128)(2,1)}, u32[]{:S(2)}) %copy-start) | copy-done | bytes 2097176
  2.9 0.0 copy-start.1
  2.9 1.0 %copy-done.1 = bf16[512,512]{1,0:T(8,128)(2,1)S(1)} copy-done((bf16[512,512]{1,0:T(8,128)(2,1)S(1)}, bf16[512,512]{1,0:T(8,128)(2,1)}, u32[]{:S(2)}) %copy-start.1) | copy-done | bytes 524312
  3.9 0.0 copy-start.2
  3.9 0.9 copy-done.2
  4.8 0.0 copy-start.3
  4.8 0.9 copy-done.3
  5.7 0.0 copy-start.4
  5.7 0.8 copy-done.4
  6.5 0.0 copy-start.5
  6.5 0.7 copy-done.5
  7.1 0.0 copy-start.6
  7.1 0.7 copy-done.6
  7.8 0.0 copy-start.7
  7.8 0.7 copy-done.7
  8.4 87.6 %shard_map.136 = (f32[8,128]{1,0:T(8,128)S(1)}, bf16[128,512]{1,0:T(8,128)(2,1)S(1)}, bf16[128,512]{1,0:T(8,128)(2,1)S(1)}, f32[8,2048]{1,0:T(8,128)S(1)}, f32[8,512]{1,0:T(8,128)S(1)}, /*index=5*/f32[32,512]{1,0:T(8,128)S(1)}) custom-call(bf16[128,512]{1,0:T(8,128)(2,1)S(1)} %bitcast.9, bf16[128,512]{1,0:T(8,128)(2,1)S(1)} %bitcast.10, ...), custom_call_target="tpu_custom_call" | custom-call | tf_op jit(solution)/shard_map/pallas_call | solution.py:621
  96.0 0.5 slice.3
  96.5 0.7 copy.21
  97.2 0.7 copy.22
  97.9 0.6 copy.23
  98.5 0.6 copy.24
  99.1 0.6 copy.25
Async XLA Ops:
  1.3 1.6 %copy-start = (bf16[512,2048]{1,0:T(8,128)(2,1)S(1)}, bf16[512,2048]{1,0:T(8,128)(2,1)}, u32[]{:S(2)}) copy-start(bf16[512,2048]{1,0:T(8,128)(2,1)} %win_ref.1) | copy-start | bytes 6291460
  2.9 1.0 %copy-start.1 = (bf16[512,512]{1,0:T(8,128)(2,1)S(1)}, bf16[512,512]{1,0:T(8,128)(2,1)}, u32[]{:S(2)}) copy-start(bf16[512,512]{1,0:T(8,128)(2,1)} %wout_ref.1) | copy-start | bytes 1572868
  3.9 0.9 copy-start.2
  4.8 0.9 copy-start.3
  5.7 0.8 copy-start.4
  6.5 0.7 copy-start.5
  7.1 0.7 copy-start.6
  7.8 0.7 copy-start.7

commit v2 on v1

v2 whole, which is shorter than its diff:
```python
import functools

import jax
import jax.numpy as jnp
from jax import lax
from jax.experimental import pallas as pl
from jax.experimental.pallas import tpu as pltpu
from jax.sharding import PartitionSpec as P

HEADS = 8
L = 512
W = 512
HIST = 4
R = 128
NB = 32
NQ = NB // HIST
NH = NB // 2
TEMP = 0.05
MESH = pl.DeviceIdType.MESH
F32 = jnp.float32
BF16 = jnp.bfloat16


def layer_norm(values):
    centered = values - jnp.mean(values, -1, keepdims=True)
    inverse = lax.rsqrt(jnp.mean(centered * centered, -1, keepdims=True) + 1e-06)
    return (centered * inverse, inverse)


def norm_back(grad, normed, inverse):
    return inverse * (
        grad
        - jnp.mean(grad, -1, keepdims=True)
        - normed * jnp.mean(grad * normed, -1, keepdims=True)
    )


def unit_rows(values):
    inverse = lax.rsqrt(jnp.sum(values * values, -1, keepdims=True) + 1e-06)
    return (values * inverse, inverse)


def unit_back(grad, unit, inverse):
    return inverse * (grad - unit * jnp.sum(unit * grad, -1, keepdims=True))


def sigmoid(values):
    return 0.5 * jnp.tanh(0.5 * values) + 0.5


def silu_slope(values):
    sigma = sigmoid(values)
    return sigma * (1.0 + values * (1.0 - sigma))


def silu(values):
    return values * sigmoid(values)


def inner_product(left, right):
    return lax.dot_general(left, right, (((1,), (1,)), ((), ())), preferred_element_type=F32)


def matmul(left, right):
    return jnp.dot(left, right, preferred_element_type=F32)


def plan(mesh):
    dp = mesh.shape["dp"]
    if dp == 64:
        return 8, 2, 4
    return dp // 2, 1, 2


def kernel(
    sizes,
    count,
    tok_hbm,
    tgt_hbm,
    tid_hbm,
    len_hbm,
    neg_hbm,
    nid_hbm,
    ncnt_hbm,
    win_hbm,
    wout_hbm,
    loss_ref,
    dtok_ref,
    dtgt_ref,
    dwin_ref,
    dwout_ref,
    dneg_ref,
    tok_ref,
    tgt_ref,
    tid_ref,
    len_ref,
    neg_ref,
    nid_ref,
    ncnt_ref,
    win_ref,
    wout_ref,
    tok_all,
    nrm_all,
    nrmf,
    proj,
    gate,
    k_all,
    v_all,
    q_all,
    slope,
    attn,
    nall,
    idz,
    idx,
    idy,
    idb,
    lcb,
    ex,
    ngo,
    ngs,
    nga,
    my_own,
    my_sib,
    da_all,
    dpq,
    dpq_r,
    dpk,
    dpk_r,
    dpo,
    dout,
    g1,
    g2,
    g3,
    l1,
    l2,
    l3,
    l4,
    lsem,
    ssem,
    rsem,
):
    nz, nyh, nx = sizes
    npl = nyh * nx
    ring = nx
    chunks = 2 * ring
    zh = nz // 2
    dp_size = nz * npl
    rw = W // dp_size
    total_events = float(dp_size * L)
    d = lax.axis_index("dp")
    h = lax.axis_index("hist")
    z = lax.div(d, npl)
    p = lax.rem(d, npl)
    yh = lax.div(p, nx)
    x = lax.rem(p, nx)
    yl = lax.div(h, 2)
    y = yh * 2 + yl
    core = lax.rem(h, 2)
    other = 1 - core
    sib = yl * 2 + other

    def hist_to(o):
        return lax.rem(h + o, HIST)

    def hist_from(o):
        return lax.rem(h + HIST - o, HIST)

    def z_to(o):
        return lax.rem(z + o, nz)

    def z_from(o):
        return lax.rem(z + nz - o, nz)

    def x_to(o):
        return lax.rem(x + o, ring)

    def x_from(o):
        return lax.rem(x + ring - o, ring)

    def y_to(o):
        return lax.rem(y + o, ring)

    def y_from(o):
        return lax.rem(y + ring - o, ring)

    def hist_dev(index):
        return {"dp": d, "hist": index}

    def z_dev(index):
        return {"dp": index * npl + p, "hist": h}

    def x_dev(index):
        return {"dp": z * npl + yh * nx + index, "hist": h}

    def y_dev(index):
        return {
            "dp": z * npl + lax.div(index, 2) * nx + x,
            "hist": lax.rem(index, 2) * 2 + core,
        }

    sends = []
    taken = [0]

    def slots(number):
        base = taken[0]
        taken[0] += number
        assert taken[0] <= count
        return base

    def send(src, dst, slot, device):
        copy = pltpu.make_async_remote_copy(
            src_ref=src,
            dst_ref=dst,
            send_sem=ssem.at[slot],
            recv_sem=rsem.at[slot],
            device_id=device,
            device_id_type=MESH,
        )
        copy.start()
        sends.append(copy)

    def recv(dst, slot):
        pltpu.make_async_remote_copy(
            src_ref=dst,
            dst_ref=dst,
            send_sem=ssem.at[slot],
            recv_sem=rsem.at[slot],
            device_id=hist_dev(sib),
            device_id_type=MESH,
        ).wait_recv()

    barrier = pltpu.get_barrier_semaphore()
    peers = (
        [hist_dev(hist_to(o)) for o in range(1, HIST)]
        + [x_dev(x_to(o)) for o in range(1, ring)]
        + [z_dev(z_to(o)) for o in range(1, nz)]
    )
    if nyh > 1:
        peers += [y_dev(lax.rem(yh + 1, nyh) * 2 + k) for k in range(2)]
    for device in peers:
        pl.semaphore_signal(barrier, inc=1, device_id=device, device_id_type=MESH)

    loads = []
    for k, (src, dst) in enumerate(
        (
            (neg_hbm, neg_ref),
            (nid_hbm, nid_ref),
            (ncnt_hbm, ncnt_ref),
            (tok_hbm, tok_ref),
            (win_hbm, win_ref),
            (wout_hbm, wout_ref),
            (tgt_hbm, tgt_ref),
            (tid_hbm, tid_ref),
            (len_hbm, len_ref),
        )
    ):
        copy = pltpu.make_async_copy(src, dst, lsem.at[k])
        copy.start()
        loads.append(copy)

    for k in range(3):
        loads[k].wait()
    n_hat, n_inv = unit_rows(neg_ref[...].astype(F32))
    rows16 = jnp.where(yl == 0, n_hat[:NH], n_hat[NH:])
    own16 = jnp.where(core == 0, rows16[:, :256], rows16[:, 256:]).astype(BF16)
    lane_at = lax.broadcasted_iota(jnp.int32, (1, 128), 1)
    own_lanes = (lane_at >= x * NB) & (lane_at < x * NB + NB)
    wide = [
        jnp.where(own_lanes, jnp.concatenate([ref[...]] * (128 // NB), axis=1), 0)
        for ref in (nid_ref, ncnt_ref)
    ]
    idz[z] = jnp.concatenate(wide + [jnp.zeros((6, 128), jnp.int32)], axis=0)

    pl.semaphore_wait(barrier, len(peers))

    s_tok = slots(HIST)
    for o in range(1, HIST):
        send(tok_hbm, tok_all.at[h], s_tok + o, hist_dev(hist_to(o)))
    upper = lax.div(z, zh)
    own_chunk = y + upper * (ring + x - y)
    own_place = x + upper * (y - x)
    own_z = lax.rem(z, zh)
    nall[core, own_chunk, own_place, own_z] = own16
    s_nz = slots(nz)
    s_iz = slots(nz)
    own_slot = nall.at[core, own_chunk, own_place, own_z]
    for o in range(1, nz):
        send(own_slot, own_slot, s_nz + o, z_dev(z_to(o)))
        send(idz.at[z], idz.at[z], s_iz + o, z_dev(z_to(o)))

    loads[3].wait()
    loads[4].wait()
    tokf = tok_ref[...].astype(F32)
    normed_f, inverse = layer_norm(tokf)
    nrmf[...] = normed_f
    normed = normed_f.astype(BF16)
    nrm_all[h] = normed
    for blk, ref in enumerate((gate, v_all.at[h], q_all.at[h], k_all.at[h])):
        cols = slice(blk * W, (blk + 1) * W)
        part = matmul(normed, win_ref[:, cols])
        proj[:, cols] = part
        ref[...] = silu(part).astype(BF16)

    for o in range(1, nz):
        src = z_from(o)
        src_upper = lax.div(src, zh)
        recv(
            nall.at[core, y + src_upper * (ring + x - y), x + src_upper * (y - x), lax.rem(src, zh)],
            s_nz + o,
        )
        recv(idz.at[src], s_iz + o)
    idx[x] = jnp.concatenate(
        [idz[k, 0:1] for k in range(nz)]
        + [jnp.zeros((8 - nz, 128), jnp.int32)] * (nz < 8)
        + [idz[k, 1:2] for k in range(nz)]
        + [jnp.zeros((8 - nz, 128), jnp.int32)] * (nz < 8),
        axis=0,
    )
    s_n2x = slots(ring)
    s_n2y = slots(ring)
    s_ix = slots(ring)
    for o in range(1, ring):
        low_half = nall.at[core, y, x]
        high_half = nall.at[core, ring + x, y]
        send(low_half, low_half, s_n2x + o, x_dev(x_to(o)))
        send(high_half, high_half, s_n2y + o, y_dev(y_to(o)))
        send(idx.at[x], idx.at[x], s_ix + o, x_dev(x_to(o)))

    for o in (1, 3, 2):
        b = hist_from(o)
        recv(tok_all.at[b], s_tok + o)
        normed_b = layer_norm(tok_all[b].astype(F32))[0].astype(BF16)
        nrm_all[b] = normed_b
        v_all[b] = silu(matmul(normed_b, win_ref[:, W : 2 * W])).astype(BF16)
        k_all[b] = silu(matmul(normed_b, win_ref[:, 3 * W :])).astype(BF16)

    for o in range(1, ring):
        recv(nall.at[core, y, x_from(o)], s_n2x + o)
        recv(nall.at[core, ring + x, y_from(o)], s_n2y + o)
        recv(idx.at[x_from(o)], s_ix + o)
    tile = idx[0]
    for k in range(1, ring):
        tile = tile + idx[k]
    idy[yh] = tile
    s_n3y = slots(ring)
    s_n3x = slots(ring)
    s_iy = slots(1)
    for o in range(1, ring):
        send(nall.at[core, y], nall.at[core, y], s_n3y + o, y_dev(y_to(o)))
        send(nall.at[core, ring + x], nall.at[core, ring + x], s_n3x + o, x_dev(x_to(o)))
    if nyh > 1:
        send(idy.at[yh], idy.at[yh], s_iy, y_dev(lax.rem(yh + 1, nyh) * 2 + yl))
    s_sib = slots(2 * ring)
    for k, own in enumerate((y, ring + x)):
        send(nall.at[core, own], nall.at[core, own], s_sib + k * ring, hist_dev(sib))

    lane = lax.broadcasted_iota(jnp.int32, (1, 128), 1)
    low = lane < 64
    half_mask = [jnp.where(low, 1.0, 0.0).astype(BF16), jnp.where(low, 0.0, 1.0).astype(BF16)]
    causal = lax.broadcasted_iota(jnp.int32, (R, L), 1) <= h * R + lax.broadcasted_iota(
        jnp.int32, (R, L), 0
    )
    scale = 0.125

    def forward_pair(n, carry):
        cols = pl.ds(pl.multiple_of(n * 128, 128), 128)
        q = q_all[h, :, cols]
        k = k_all[:, :, cols].reshape(L, 128)
        v = v_all[:, :, cols].reshape(L, 128)
        halves = []
        for e in range(2):
            s = inner_product(q * half_mask[e], k) * scale
            sigma = sigmoid(s)
            w = jnp.where(causal, s * sigma * (1.0 / L), 0.0).astype(BF16)
            slope[2 * n + e] = jnp.where(
                causal, sigma * (1.0 + s * (1.0 - sigma)) * (scale / L), 0.0
            )
            halves.append(matmul(w, v))
        attn[:, cols] = jnp.where(low, halves[0], halves[1]).astype(BF16)
        return carry

    lax.fori_loop(0, HEADS // 2, forward_pair, 0)

    for k in range(5, 9):
        loads[k].wait()
    attn_normed, attn_inv = layer_norm(attn[...].astype(F32))
    gate_f = gate[...].astype(F32)
    mixed = (attn_normed * gate_f).astype(BF16)
    my_own[:, :W] = mixed
    output = tok_ref[...].astype(F32) + matmul(mixed, wout_ref[...])
    y_hat, y_inv = unit_rows(output)
    y_hat_b = y_hat.astype(BF16)
    my_own[:, W:] = y_hat_b
    t_hat, t_inv = unit_rows(tgt_ref[...].astype(F32))
    pos_col = jnp.sum(y_hat * t_hat, -1, keepdims=True) / TEMP
    pos_row = jnp.broadcast_to(pos_col, (R, 128)).T[0:1, :]

    for o in range(1, ring):
        for k, (src, base) in enumerate(((y_from(o), s_n3y), (ring + x_from(o), s_n3x))):
            recv(nall.at[core, src], base + o)
            send(nall.at[core, src], nall.at[core, src], s_sib + k * ring + o, hist_dev(sib))
    s_my = slots(1)
    send(my_own, my_sib, s_my, hist_dev(sib))
    if nyh > 1:
        recv(idy.at[lax.rem(yh + 1, nyh)], s_iy)
    for a in range(nyh):
        ids = idy[a, :8].astype(F32)
        logs = jnp.log(jnp.maximum(idy[a, 8:].astype(F32), 1.0))
        turned = jnp.concatenate([ids, logs, jnp.zeros((112, 128), F32)], axis=0).T
        for b in range(nx):
            for c in range(2):
                rows = turned[b * NB + c * NH : b * NB + (c + 1) * NH]
                for k in range(nz):
                    if k < zh:
                        chunk, place = 2 * a + c, b
                    else:
                        chunk, place = ring + b, 2 * a + c
                    at = pl.ds((place * zh + k % zh) * NH, NH)
                    idb[chunk, at] = jnp.broadcast_to(rows[:, k : k + 1], (NH, 128))
                    lcb[chunk, at] = jnp.broadcast_to(rows[:, 8 + k : 9 + k], (NH, 128))
    for o in range(ring):
        recv(nall.at[other, y_from(o)], s_sib + o)
        recv(nall.at[other, ring + x_from(o)], s_sib + ring + o)

    span = ring * zh * NH
    tid_row = tid_ref[...].astype(F32)

    def logits_chunk(c, acc):
        lg = inner_product(nall[0, c].reshape(span, 256), y_hat_b[:, :256]) + inner_product(
            nall[1, c].reshape(span, 256), y_hat_b[:, 256:]
        )
        lg = lg * (1.0 / TEMP) - lcb[c]
        value = jnp.where(idb[c] != tid_row, jnp.exp(lg), 0.0)
        ex[c] = value
        return acc + jnp.sum(value.reshape(span // 8, 8, 128), 0)

    acc = lax.fori_loop(0, chunks, logits_chunk, jnp.zeros((8, 128), F32))
    total = jnp.exp(pos_row) + jnp.sum(acc, 0, keepdims=True)
    position = h * R + lax.broadcasted_iota(jnp.int32, (1, 128), 1)
    valid = jnp.where(position < len_ref[...], 1.0, 0.0)
    pg_row = valid * (jnp.exp(pos_row) / total - 1.0) / TEMP
    pg = jnp.broadcast_to(pg_row, (128, 128)).T[:, 0:1]
    scale_row = valid / (total * TEMP)

    def grad_chunk(c, carry):
        g = ex[c] * scale_row
        ngo[c] = g.astype(BF16)
        g4 = g.reshape(span // NH, 2, NQ, 128)
        for q in range(2):
            ngs[q, c] = g4[:, q].reshape(span // 2, 128).astype(BF16)
        return carry

    lax.fori_loop(0, chunks, grad_chunk, 0)
    ng = ngo[...].reshape(dp_size * NB, 128).T
    d_hat = pg * t_hat + jnp.concatenate(
        [matmul(ng, nall[c].reshape(dp_size * NB, 256)) for c in range(2)], axis=1
    )
    d_out = unit_back(d_hat, y_hat, y_inv)
    d_out_b = d_out.astype(BF16)
    d_mixed = inner_product(d_out_b, wout_ref[...])
    da_all[h] = norm_back(d_mixed * gate_f, attn_normed, attn_inv).astype(BF16)
    s_da = slots(HIST)
    for o in range(1, HIST):
        send(da_all.at[h], da_all.at[h], s_da + o, hist_dev(hist_to(o)))
    s_ng = slots(1)
    send(ngs.at[other], nga, s_ng, hist_dev(sib))
    dout[...] = d_out
    dtgt_ref[...] = unit_back(pg * y_hat, t_hat, t_inv).astype(BF16)
    d_gate = (d_mixed * attn_normed * silu_slope(proj[:, :W])).astype(BF16)
    dpo[:, :W] = d_gate
    for n in range(HIST):
        cols = slice(n * 128, (n + 1) * 128)
        dpq[n % 2, n // 2, :, 0:128] = d_out_b[:, cols]
        dpq[n % 2, n // 2, :, 128:256] = d_gate[:, cols]

    loss = jnp.sum(valid * (jnp.log(total) - pos_row), -1, keepdims=True)
    l1[x] = jnp.broadcast_to(loss, (8, 128))
    s_l1 = slots(ring)
    for o in range(1, ring):
        send(l1.at[x], l1.at[x], s_l1 + o, x_dev(x_to(o)))

    def query_pair(n, carry):
        cols = pl.ds(pl.multiple_of(n * 128, 128), 128)
        da = da_all[h, :, cols]
        k = k_all[:, :, cols].reshape(L, 128)
        v = v_all[:, :, cols].reshape(L, 128)
        halves = []
        for e in range(2):
            dw = inner_product(da * half_mask[e], v)
            halves.append(matmul((dw * slope[2 * n + e]).astype(BF16), k))
        dq = jnp.where(low, halves[0], halves[1]).astype(BF16).astype(F32)
        at = pl.ds(pl.multiple_of(2 * W + n * 128, 128), 128)
        piece = (dq * silu_slope(proj[:, at])).astype(BF16)
        dpo[:, at] = piece
        dpq[lax.rem(n, 2), lax.div(n, 2), :, 256:384] = piece
        return carry

    lax.fori_loop(0, HEADS // 2, query_pair, 0)
    s_dq = slots(1)
    send(dpq.at[other], dpq_r, s_dq, hist_dev(sib))

    def leg1(group):
        src, arrived = group[0], group[1]
        base = slots(2 * ring)
        for o in range(1, ring):
            send(src.at[y_to(o)], arrived.at[0, o], base + o, y_dev(y_to(o)))
            send(src.at[ring + x_to(o)], arrived.at[1, o], base + ring + o, x_dev(x_to(o)))
        return base

    def leg2(group, base):
        src, arrived, mid, arrived2 = group[:4]
        out = slots(2 * ring)
        for part, own in enumerate((y, ring + x)):
            total = src[own].astype(F32)
            for o in range(1, ring):
                recv(arrived.at[part, o], base + part * ring + o)
                total = total + arrived[part, o].astype(F32)
            mid[part] = total.astype(BF16).reshape(mid.shape[1:])
            for o in range(1, ring):
                to, device = (x_to(o), x_dev(x_to(o))) if part == 0 else (y_to(o), y_dev(y_to(o)))
                send(mid.at[part, to], arrived2.at[part, o], out + part * ring + o, device)
        return out

    def leg3(group, base):
        mid, arrived2, zs, zr = group[2:6]
        for part, own in enumerate((x, y)):
            total = mid[part, own].astype(F32)
            for o in range(1, ring):
                recv(arrived2.at[part, o], base + part * ring + o)
                total = total + arrived2[part, o].astype(F32)
            zs[part * zh : (part + 1) * zh] = total.reshape((zh,) + zs.shape[1:])
        out = slots(nz)
        for o in range(1, nz):
            send(zs.at[z_to(o)], zr.at[o], out + o, z_dev(z_to(o)))
        return out

    def leg4(group, base):
        zs, zr, eh = group[4:]
        total = zs[z]
        for o in range(1, nz):
            recv(zr.at[o], base + o)
            total = total + zr[o]
        eh[h] = total
        out = slots(HIST)
        for o in range(1, HIST):
            send(eh.at[h], eh.at[h], out + o, hist_dev(hist_to(o)))
        return out

    def arrive(group, base):
        for o in range(1, HIST):
            recv(group[6].at[hist_from(o)], base + o)

    def spread(result, k, group, c0):
        width = result.shape[1]
        for a in range(nyh):
            for b in range(nx):
                for half in range(2):
                    block = jnp.concatenate(
                        [
                            result[((half * zh + j) * npl + a * nx + b) * rw :][:rw]
                            for j in range(zh)
                        ],
                        axis=0,
                    ).astype(BF16)
                    chunk, place = (2 * a + k, b) if half == 0 else (ring + b, 2 * a + k)
                    group[0][chunk, place * zh * rw : (place + 1) * zh * rw, c0 : c0 + width] = block

    recv(my_sib, s_my)
    recv(nga, s_ng)

    def neg_chunk(c, carry):
        left = jnp.concatenate([ngs[core, c], nga[c]], axis=1)
        right = jnp.concatenate([my_own[:, W:], my_sib[:, W:]], axis=0)
        g1[0][c] = matmul(left, right).astype(BF16)
        return carry

    lax.fori_loop(0, chunks, neg_chunk, 0)
    t1 = leg1(g1)

    mixed_t = jnp.concatenate([my_own[:, :W], my_sib[:, :W]], axis=0).T
    normed_t = jnp.concatenate([nrm_all[h], nrm_all[sib]], axis=0).T
    recv(dpq_r, s_dq)
    for k in range(2):
        right = jnp.concatenate([dpq[core, k], dpq_r[k]], axis=0)
        spread(matmul(mixed_t, right[:, :128]), k, g2, 0)
        spread(matmul(normed_t, right[:, 128:]), k, g2, 128)
    t2 = leg1(g2)

    for o in range(1, HIST):
        b = hist_from(o)
        q_all[b] = silu(matmul(nrm_all[b], win_ref[:, 2 * W : 3 * W])).astype(BF16)

    for o in range(1, ring):
        recv(l1.at[x_from(o)], s_l1 + o)
    part = l1[0]
    for k in range(1, ring):
        part = part + l1[k]
    l2[y] = part
    s_l2 = slots(ring)
    for o in range(1, ring):
        send(l2.at[y], l2.at[y], s_l2 + o, y_dev(y_to(o)))

    for o in range(1, HIST):
        recv(da_all.at[hist_from(o)], s_da + o)
    causal_t = lax.broadcasted_iota(jnp.int32, (R, L), 1) >= h * R + lax.broadcasted_iota(
        jnp.int32, (R, L), 0
    )

    def key_pair(n, carry):
        cols = pl.ds(pl.multiple_of(n * 128, 128), 128)
        k = k_all[h, :, cols]
        v = v_all[h, :, cols]
        q = q_all[:, :, cols].reshape(L, 128)
        da = da_all[:, :, cols].reshape(L, 128)
        dks, dvs = [], []
        for e in range(2):
            s = inner_product(k * half_mask[e], q) * scale
            sigma = sigmoid(s)
            w = jnp.where(causal_t, s * sigma * (1.0 / L), 0.0).astype(BF16)
            dw = inner_product(v * half_mask[e], da)
            ds = jnp.where(
                causal_t, dw * (sigma * (1.0 + s * (1.0 - sigma))) * (scale / L), 0.0
            ).astype(BF16)
            dks.append(matmul(ds, q))
            dvs.append(matmul(w, da))
        for at, parts, place in ((W, dvs, 0), (3 * W, dks, 128)):
            grad = jnp.where(low, parts[0], parts[1]).astype(BF16).astype(F32)
            at = pl.ds(pl.multiple_of(at + n * 128, 128), 128)
            piece = (grad * silu_slope(proj[:, at])).astype(BF16)
            dpo[:, at] = piece
            dpk[lax.rem(n, 2), lax.div(n, 2), :, place : place + 128] = piece
        return carry

    lax.fori_loop(0, HEADS // 2, key_pair, 0)
    s_dk = slots(1)
    send(dpk.at[other], dpk_r, s_dk, hist_dev(sib))

    t1 = leg2(g1, t1)
    recv(dpk_r, s_dk)
    for k in range(2):
        right = jnp.concatenate([dpk[core, k], dpk_r[k]], axis=0)
        spread(matmul(normed_t, right), k, g3, 0)
    t3 = leg1(g3)
    t2 = leg2(g2, t2)

    for o in range(1, ring):
        recv(l2.at[y_from(o)], s_l2 + o)
    part = l2[0]
    for k in range(1, ring):
        part = part + l2[k]
    l3[z] = part
    s_l3 = slots(nz)
    for o in range(1, nz):
        send(l3.at[z], l3.at[z], s_l3 + o, z_dev(z_to(o)))

    grad = inner_product(dpo[...], win_ref[...])
    dtok_ref[...] = (dout[...] + norm_back(grad, nrmf[...], inverse)).astype(BF16)

    t1 = leg3(g1, t1)
    t3 = leg2(g3, t3)
    t2 = leg3(g2, t2)
    t1 = leg4(g1, t1)
    t3 = leg3(g3, t3)
    for o in range(1, nz):
        recv(l3.at[z_from(o)], s_l3 + o)
    part = l3[0]
    for k in range(1, nz):
        part = part + l3[k]
    l4[core] = part
    s_l4 = slots(1)
    send(l4.at[core], l4.at[core], s_l4, hist_dev(sib))
    t2 = leg4(g2, t2)
    arrive(g1, t1)
    d_nhat = g1[6][...].reshape(NB, W)
    dneg_ref[...] = unit_back(d_nhat, n_hat, n_inv) / total_events
    t3 = leg4(g3, t3)
    recv(l4.at[other], s_l4)
    loss_ref[...] = (l4[0] + l4[1]) / total_events
    arrive(g2, t2)
    for k in range(HIST):
        cols = slice(k * 128, (k + 1) * 128)
        dwout_ref[:, cols] = g2[6][k, :, 0:128] / total_events
        dwin_ref[:, cols] = g2[6][k, :, 128:256] / total_events
        dwin_ref[:, 2 * W + k * 128 : 2 * W + (k + 1) * 128] = g2[6][k, :, 256:384] / total_events
    arrive(g3, t3)
    for k in range(HIST):
        dwin_ref[:, W + k * 128 : W + (k + 1) * 128] = g3[6][k, :, 0:128] / total_events
        dwin_ref[:, 3 * W + k * 128 : 3 * W + (k + 1) * 128] = g3[6][k, :, 128:256] / total_events
    for copy in sends:
        copy.wait_send()


def local(sizes, *args):
    tokens, targets, target_ids, lengths, negatives, negative_ids, counts, w_in, w_out = args
    nz, nyh, nx = sizes
    npl = nyh * nx
    dp_size = nz * npl
    rw = W // dp_size
    ring = nx
    assert ring == 2 * nyh
    zh = nz // 2
    chunks = 2 * ring
    span = ring * zh * NH
    vmem = pltpu.VMEM
    count = 256

    def group(rows, width):
        block = ring * zh * rows
        return (
            vmem((chunks, block, width), BF16),
            vmem((2, ring, block, width), BF16),
            vmem((2, ring, zh * rows, width), BF16),
            vmem((2, ring, zh * rows, width), BF16),
            vmem((nz, rows, width), F32),
            vmem((nz, rows, width), F32),
            vmem((HIST, rows, width), F32),
        )

    scratch = [
        vmem((R, W), BF16),
        vmem((R, W), BF16),
        vmem((1, R), jnp.int32),
        vmem((1, 1), jnp.int32),
        vmem((NB, W), BF16),
        vmem((1, NB), jnp.int32),
        vmem((1, NB), jnp.int32),
        vmem((W, 4 * W), BF16),
        vmem((W, W), BF16),
        vmem((HIST, R, W), BF16),
        vmem((HIST, R, W), BF16),
        vmem((R, W), F32),
        vmem((R, 4 * W), F32),
        vmem((R, W), BF16),
        vmem((HIST, R, W), BF16),
        vmem((HIST, R, W), BF16),
        vmem((HIST, R, W), BF16),
        vmem((HEADS, R, L), F32),
        vmem((R, W), BF16),
        vmem((2, chunks, ring, zh, NH, 256), BF16),
        vmem((nz, 8, 128), jnp.int32),
        vmem((ring, 16, 128), jnp.int32),
        vmem((nyh, 16, 128), jnp.int32),
        vmem((chunks, span, 128), F32),
        vmem((chunks, span, 128), F32),
        vmem((chunks, span, 128), F32),
        vmem((chunks, span, 128), BF16),
        vmem((2, chunks, span // 2, 128), BF16),
        vmem((chunks, span // 2, 128), BF16),
        vmem((R, 2 * W), BF16),
        vmem((R, 2 * W), BF16),
        vmem((HIST, R, W), BF16),
        vmem((2, 2, R, 384), BF16),
        vmem((2, R, 384), BF16),
        vmem((2, 2, R, 256), BF16),
        vmem((2, R, 256), BF16),
        vmem((R, 4 * W), BF16),
        vmem((R, W), F32),
        group(NQ, W),
        group(rw, 384),
        group(rw, 256),
        vmem((ring, 8, 128), F32),
        vmem((ring, 8, 128), F32),
        vmem((nz, 8, 128), F32),
        vmem((2, 8, 128), F32),
        pltpu.SemaphoreType.DMA((9,)),
        pltpu.SemaphoreType.DMA((count,)),
        pltpu.SemaphoreType.DMA((count,)),
    ]
    shape = jax.ShapeDtypeStruct
    outs = pl.pallas_call(
        functools.partial(kernel, sizes, count),
        out_shape=[
            shape((8, 128), F32),
            shape((R, W), BF16),
            shape((R, W), BF16),
            shape((rw, 4 * W), F32),
            shape((rw, W), F32),
            shape((NB, W), F32),
        ],
        in_specs=[pl.BlockSpec(memory_space=pltpu.HBM)] * 9,
        out_specs=[pl.BlockSpec(memory_space=pltpu.VMEM)] * 6,
        scratch_shapes=scratch,
        compiler_params=pltpu.CompilerParams(
            collective_id=0, has_side_effects=True, vmem_limit_bytes=48 * 1024 * 1024
        ),
    )(
        tokens.reshape(R, W),
        targets.reshape(R, W),
        target_ids,
        lengths.reshape(1, 1),
        negatives,
        negative_ids.reshape(1, NB),
        counts.reshape(1, NB),
        w_in,
        w_out,
    )
    return (
        outs[0][0, 0],
        outs[1].reshape(1, R, W),
        outs[2].reshape(1, R, W),
        outs[3],
        outs[4],
        outs[5],
    )


def solution(mesh):
    in_specs = (
        P("dp", "hist", None),
        P("dp", "hist", None),
        P("dp", "hist"),
        P("dp"),
        P("dp", None),
        P("dp"),
        P("dp"),
        P(),
        P(),
    )
    out_specs = (
        P(),
        P("dp", "hist", None),
        P("dp", "hist", None),
        P("dp", None),
        P("dp", None),
        P("dp", None),
    )
    return jax.shard_map(
        functools.partial(local, plan(mesh)),
        mesh=mesh,
        in_specs=in_specs,
        out_specs=out_specs,
        check_vma=False,
    )
```

time: 100 us -> 82.9 us (0.83)
  Pallas kernels: 87.6 us -> 70.5 us
    pallas_call x1, Pallas kernels: 87.6 us -> 70.5 us  [local(): pl.pallas_call(functools.partial(kernel, sizes, count), out_shape=[shape(...]
where the time goes in v2:
time: 82.9 us; the launch traced here: 82.6 us
  Pallas kernels  70.5 us (85%)
  local copies, waits for them, and re-layouts  10.8 us (13%)
  between operations  1.31 us (2%)
    pallas_call x1, Pallas kernels, local(): pl.pallas_call(functools.partial(kernel, sizes, count), out_shape=[shape(...  70.5 us
    unnamed x21, local copies, waits for them, and re-layouts  10.3 us

profile of v2, /device:TPU:1, one launch (start us, length us, event | category | flops | bytes accessed | tf_op | source)
XLA Modules:
  0.0 82.6 jit_solution(17698719942107518455)
XLA Ops:
  1.3 0.0 copy-start
  1.3 1.6 %copy-done = bf16[512,2048]{1,0:T(8,128)(2,1)S(1)} copy-done((bf16[512,2048]{1,0:T(8,128)(2,1)S(1)}, bf16[512,2048]{1,0:T(8,128)(2,1)}, u32[]{:S(2)}) %copy-start) | copy-done | bytes 2097176
  2.9 0.0 copy-start.1
  2.9 1.0 %copy-done.1 = bf16[512,512]{1,0:T(8,128)(2,1)S(1)} copy-done((bf16[512,512]{1,0:T(8,128)(2,1)S(1)}, bf16[512,512]{1,0:T(8,128)(2,1)}, u32[]{:S(2)}) %copy-start.1) | copy-done | bytes 524312
  3.9 0.0 copy-start.2
  3.9 0.9 %copy-done.2 = bf16[1,128,512]{2,1,0:T(8,128)(2,1)S(1)} copy-done((bf16[1,128,512]{2,1,0:T(8,128)(2,1)S(1)}, bf16[1,128,512]{2,1,0:T(8,128)(2,1)}, u32[]{:S(2)}) %copy-start.2) | copy-done | bytes 131096
  4.8 0.0 copy-start.3
  4.8 0.9 %copy-done.3 = bf16[1,128,512]{2,1,0:T(8,128)(2,1)S(1)} copy-done((bf16[1,128,512]{2,1,0:T(8,128)(2,1)S(1)}, bf16[1,128,512]{2,1,0:T(8,128)(2,1)}, u32[]{:S(2)}) %copy-start.3) | copy-done | bytes 131096
  5.7 0.0 copy-start.4
  5.7 0.8 copy-done.4
  6.5 0.0 copy-start.5
  6.5 0.7 copy-done.5
  7.1 0.0 copy-start.6
  7.1 0.7 copy-done.6
  7.8 0.0 copy-start.7
  7.8 0.7 copy-done.7
  8.4 70.5 %shard_map.136 = (f32[8,128]{1,0:T(8,128)S(1)}, bf16[128,512]{1,0:T(8,128)(2,1)S(1)}, bf16[128,512]{1,0:T(8,128)(2,1)S(1)}, f32[8,2048]{1,0:T(8,128)S(1)}, f32[8,512]{1,0:T(8,128)S(1)}, /*index=5*/f32[32,512]{1,0:T(8,128)S(1)}) custom-call(bf16[128,512]{1,0:T(8,128)(2,1)S(1)} %bitcast.9, bf16[128,512]{1,0:T(8,128)(2,1)S(1)} %bitcast.10, ...), custom_call_target="tpu_custom_call" | custom-call | tf_op jit(solution)/shard_map/pallas_call | solution.py:770
  78.9 0.5 slice.3
  79.5 0.7 copy.21
  80.1 0.7 copy.22
  80.8 0.6 copy.23
  81.4 0.6 copy.24
  82.0 0.6 copy.25
Async XLA Ops:
  1.3 1.6 %copy-start = (bf16[512,2048]{1,0:T(8,128)(2,1)S(1)}, bf16[512,2048]{1,0:T(8,128)(2,1)}, u32[]{:S(2)}) copy-start(bf16[512,2048]{1,0:T(8,128)(2,1)} %win_hbm.1) | copy-start | bytes 6291460
  2.9 1.0 %copy-start.1 = (bf16[512,512]{1,0:T(8,128)(2,1)S(1)}, bf16[512,512]{1,0:T(8,128)(2,1)}, u32[]{:S(2)}) copy-start(bf16[512,512]{1,0:T(8,128)(2,1)} %wout_hbm.1) | copy-start | bytes 1572868
  3.9 0.9 %copy-start.2 = (bf16[1,128,512]{2,1,0:T(8,128)(2,1)S(1)}, bf16[1,128,512]{2,1,0:T(8,128)(2,1)}, u32[]{:S(2)}) copy-start(bf16[1,128,512]{2,1,0:T(8,128)(2,1)} %param.9) | copy-start | bytes 393220
  4.8 0.9 %copy-start.3 = (bf16[1,128,512]{2,1,0:T(8,128)(2,1)S(1)}, bf16[1,128,512]{2,1,0:T(8,128)(2,1)}, u32[]{:S(2)}) copy-start(bf16[1,128,512]{2,1,0:T(8,128)(2,1)} %param.10) | copy-start | bytes 393220
  5.7 0.8 copy-start.4
  6.5 0.7 copy-start.5
  7.1 0.7 copy-start.6
  7.8 0.7 copy-start.7

commit v3 on v2

--- a/solution.py
+++ b/solution.py
@@ -17,6 +17,7 @@
 NH = NB // 2
 TEMP = 0.05
 MESH = pl.DeviceIdType.MESH
+VMEM_LIMIT = 64 * 1024 * 1024
 F32 = jnp.float32
 BF16 = jnp.bfloat16
 
@@ -84,6 +85,12 @@
     ncnt_hbm,
     win_hbm,
     wout_hbm,
+    loss_hbm,
+    dtok_hbm,
+    dtgt_hbm,
+    dwin_hbm,
+    dwout_hbm,
+    dneg_hbm,
     loss_ref,
     dtok_ref,
     dtgt_ref,
@@ -136,6 +143,7 @@
     l3,
     l4,
     lsem,
+    osem,
     ssem,
     rsem,
 ):
@@ -228,6 +236,13 @@
             device_id=hist_dev(sib),
             device_id_type=MESH,
         ).wait_recv()
+
+    stores = []
+
+    def store(src, dst):
+        copy = pltpu.make_async_copy(src, dst, osem.at[len(stores)])
+        copy.start()
+        stores.append(copy)
 
     barrier = pltpu.get_barrier_semaphore()
     peers = (
@@ -437,7 +452,7 @@
     acc = lax.fori_loop(0, chunks, logits_chunk, jnp.zeros((8, 128), F32))
     total = jnp.exp(pos_row) + jnp.sum(acc, 0, keepdims=True)
     position = h * R + lax.broadcasted_iota(jnp.int32, (1, 128), 1)
-    valid = jnp.where(position < len_ref[...], 1.0, 0.0)
+    valid = jnp.where(position < len_ref[0], 1.0, 0.0)
     pg_row = valid * (jnp.exp(pos_row) / total - 1.0) / TEMP
     pg = jnp.broadcast_to(pg_row, (128, 128)).T[:, 0:1]
     scale_row = valid / (total * TEMP)
@@ -466,6 +481,7 @@
     send(ngs.at[other], nga, s_ng, hist_dev(sib))
     dout[...] = d_out
     dtgt_ref[...] = unit_back(pg * y_hat, t_hat, t_inv).astype(BF16)
+    store(dtgt_ref, dtgt_hbm)
     d_gate = (d_mixed * attn_normed * silu_slope(proj[:, :W])).astype(BF16)
     dpo[:, :W] = d_gate
     for n in range(HIST):
@@ -655,6 +671,7 @@
 
     grad = inner_product(dpo[...], win_ref[...])
     dtok_ref[...] = (dout[...] + norm_back(grad, nrmf[...], inverse)).astype(BF16)
+    store(dtok_ref, dtok_hbm)
 
     t1 = leg3(g1, t1)
     t3 = leg2(g3, t3)
@@ -673,21 +690,40 @@
     arrive(g1, t1)
     d_nhat = g1[6][...].reshape(NB, W)
     dneg_ref[...] = unit_back(d_nhat, n_hat, n_inv) / total_events
+    store(dneg_ref, dneg_hbm)
     t3 = leg4(g3, t3)
     recv(l4.at[other], s_l4)
-    loss_ref[...] = (l4[0] + l4[1]) / total_events
+    loss_ref[...] = (l4[0] + l4[1])[0:1, 0:1] / total_events
+    store(loss_ref, loss_hbm)
     arrive(g2, t2)
     for k in range(HIST):
         cols = slice(k * 128, (k + 1) * 128)
         dwout_ref[:, cols] = g2[6][k, :, 0:128] / total_events
         dwin_ref[:, cols] = g2[6][k, :, 128:256] / total_events
         dwin_ref[:, 2 * W + k * 128 : 2 * W + (k + 1) * 128] = g2[6][k, :, 256:384] / total_events
+    store(dwout_ref, dwout_hbm)
     arrive(g3, t3)
     for k in range(HIST):
         dwin_ref[:, W + k * 128 : W + (k + 1) * 128] = g3[6][k, :, 0:128] / total_events
         dwin_ref[:, 3 * W + k * 128 : 3 * W + (k + 1) * 128] = g3[6][k, :, 128:256] / total_events
+    store(dwin_ref, dwin_hbm)
     for copy in sends:
         copy.wait_send()
+    for copy in stores:
+        copy.wait()
+
+
+def hand_over(*refs):
+    sources, results, staged, sems = refs[:6], refs[6:12], refs[12:18], refs[18]
+    loads = [pltpu.make_async_copy(sources[k], staged[k], sems.at[k]) for k in range(6)]
+    stores = [pltpu.make_async_copy(staged[k], results[k], sems.at[6 + k]) for k in range(6)]
+    for copy in loads:
+        copy.start()
+    for load, copy in zip(loads, stores):
+        load.wait()
+        copy.start()
+    for copy in stores:
+        copy.wait()
 
 
 def local(sizes, *args):
@@ -717,10 +753,16 @@
         )
 
     scratch = [
+        vmem((1, 1), F32),
+        vmem((R, W), BF16),
+        vmem((R, W), BF16),
+        vmem((rw, 4 * W), F32),
+        vmem((rw, W), F32),
+        vmem((NB, W), F32),
         vmem((R, W), BF16),
         vmem((R, W), BF16),
         vmem((1, R), jnp.int32),
-        vmem((1, 1), jnp.int32),
+        pltpu.SMEM((1,), jnp.int32),
         vmem((NB, W), BF16),
         vmem((1, NB), jnp.int32),
         vmem((1, NB), jnp.int32),
@@ -763,39 +805,50 @@
         vmem((nz, 8, 128), F32),
         vmem((2, 8, 128), F32),
         pltpu.SemaphoreType.DMA((9,)),
+        pltpu.SemaphoreType.DMA((6,)),
         pltpu.SemaphoreType.DMA((count,)),
         pltpu.SemaphoreType.DMA((count,)),
     ]
     shape = jax.ShapeDtypeStruct
+    shapes = [
+        shape((1, 1), F32),
+        shape((R, W), BF16),
+        shape((R, W), BF16),
+        shape((rw, 4 * W), F32),
+        shape((rw, W), F32),
+        shape((NB, W), F32),
+    ]
     outs = pl.pallas_call(
         functools.partial(kernel, sizes, count),
-        out_shape=[
-            shape((8, 128), F32),
-            shape((R, W), BF16),
-            shape((R, W), BF16),
-            shape((rw, 4 * W), F32),
-            shape((rw, W), F32),
-            shape((NB, W), F32),
-        ],
+        out_shape=shapes,
         in_specs=[pl.BlockSpec(memory_space=pltpu.HBM)] * 9,
-        out_specs=[pl.BlockSpec(memory_space=pltpu.VMEM)] * 6,
+        out_specs=[pl.BlockSpec(memory_space=pltpu.HBM)] * 6,
         scratch_shapes=scratch,
         compiler_params=pltpu.CompilerParams(
-            collective_id=0, has_side_effects=True, vmem_limit_bytes=48 * 1024 * 1024
+            collective_id=0, has_side_effects=True, vmem_limit_bytes=VMEM_LIMIT
         ),
     )(
         tokens.reshape(R, W),
         targets.reshape(R, W),
         target_ids,
-        lengths.reshape(1, 1),
+        lengths,
         negatives,
         negative_ids.reshape(1, NB),
         counts.reshape(1, NB),
         w_in,
         w_out,
     )
+    outs = pl.pallas_call(
+        hand_over,
+        out_shape=shapes,
+        in_specs=[pl.BlockSpec(memory_space=pl.ANY)] * 6,
+        out_specs=[pl.BlockSpec(memory_space=pl.ANY)] * 6,
+        scratch_shapes=[vmem(item.shape, item.dtype) for item in shapes]
+        + [pltpu.SemaphoreType.DMA((12,))],
+        compiler_params=pltpu.CompilerParams(vmem_limit_bytes=VMEM_LIMIT),
+    )(*outs)
     return (
-        outs[0][0, 0],
+        outs[0].reshape(()),
         outs[1].reshape(1, R, W),
         outs[2].reshape(1, R, W),
         outs[3],

time: 82.9 us -> 75.3 us (0.908)
  local copies, waits for them, and re-layouts: 10.8 us -> 0 us
  Pallas kernels: 70.5 us -> 73.9 us
    unnamed x21 -> x0, local copies, waits for them, and re-layouts: 10.3 us -> none
    pallas_call x1 -> x2, Pallas kernels: 70.5 us -> 73.9 us  [the longest x1 71.5 us: local(): pl.pallas_call(functools.partial(kernel, sizes, count), out_shape=shapes,...]
where the time goes in v3:
time: 75.3 us; the launch traced here: 75.2 us
  Pallas kernels  73.9 us (98%)
  between operations  1.29 us (2%)
    pallas_call x1, Pallas kernels, local(): pl.pallas_call(functools.partial(kernel, sizes, count), out_shape=shapes,...  71.5 us
    pallas_call x1, Pallas kernels, local(): pl.pallas_call(hand_over, out_shape=shapes, in_specs=[pl.BlockSpec(memory...  2.35 us

profile of v3, /device:TPU:1, one launch (start us, length us, event | category | flops | bytes accessed | tf_op | source)
XLA Modules:
  0.0 75.2 jit_solution(8339931054259525514)
XLA Ops:
  1.3 71.5 %shard_map.136 = (f32[1,1]{1,0:T(1,128)}, bf16[128,512]{1,0:T(8,128)(2,1)}, bf16[128,512]{1,0:T(8,128)(2,1)}, f32[8,2048]{1,0:T(8,128)}, f32[8,512]{1,0:T(8,128)}, /*index=5*/f32[32,512]{1,0:T(8,128)}) custom-call(bf16[128,512]{1,0:T(8,128)(2,1)} %bitcast.7, bf16[128,512]{1,0:T(8,128)(2,1)} %bitcast.8, s32[1,128]{1,0:T(1,128)} %tid_hbm.1, ...), custom_call_target="tpu_custom_call" | custom-call | tf_op jit(solution)/shard_map/pallas_call | solution.py:821
  72.8 2.3 %shard_map.137 = (f32[1,1]{1,0:T(1,128)}, bf16[128,512]{1,0:T(8,128)(2,1)}, bf16[128,512]{1,0:T(8,128)(2,1)}, f32[8,2048]{1,0:T(8,128)}, f32[8,512]{1,0:T(8,128)}, /*index=5*/f32[32,512]{1,0:T(8,128)}) custom-call(f32[1,1]{1,0:T(1,128)} %get-tuple-element.18.refs_0_, bf16[128,512]{1,0:T(8,128)(2,1)} %get-tuple-element.19.refs_1_, ...), custom_call_target="tpu_custom_call" | custom-call | tf_op jit(solution)/shard_map/pallas_call | solution.py:841

commit v4 on v3

--- a/solution.py
+++ b/solution.py
@@ -115,6 +115,8 @@
     v_all,
     q_all,
     slope,
+    slope_t,
+    weights_t,
     attn,
     nall,
     idz,
@@ -166,6 +168,8 @@
     core = lax.rem(h, 2)
     other = 1 - core
     sib = yl * 2 + other
+    partner = (1 - yl) * 2 + core
+    cross = (1 - yl) * 2 + other
 
     def hist_to(o):
         return lax.rem(h + o, HIST)
@@ -288,9 +292,6 @@
 
     pl.semaphore_wait(barrier, len(peers))
 
-    s_tok = slots(HIST)
-    for o in range(1, HIST):
-        send(tok_hbm, tok_all.at[h], s_tok + o, hist_dev(hist_to(o)))
     upper = lax.div(z, zh)
     own_chunk = y + upper * (ring + x - y)
     own_place = x + upper * (y - x)
@@ -302,6 +303,9 @@
     for o in range(1, nz):
         send(own_slot, own_slot, s_nz + o, z_dev(z_to(o)))
         send(idz.at[z], idz.at[z], s_iz + o, z_dev(z_to(o)))
+    s_tok = slots(3)
+    send(tok_hbm, tok_all.at[h], s_tok, hist_dev(partner))
+    send(tok_hbm, tok_all.at[h], s_tok + 1, hist_dev(sib))
 
     loads[3].wait()
     loads[4].wait()
@@ -341,13 +345,17 @@
         send(high_half, high_half, s_n2y + o, y_dev(y_to(o)))
         send(idx.at[x], idx.at[x], s_ix + o, x_dev(x_to(o)))
 
-    for o in (1, 3, 2):
-        b = hist_from(o)
-        recv(tok_all.at[b], s_tok + o)
+    def keys_values(b):
         normed_b = layer_norm(tok_all[b].astype(F32))[0].astype(BF16)
         nrm_all[b] = normed_b
         v_all[b] = silu(matmul(normed_b, win_ref[:, W : 2 * W])).astype(BF16)
         k_all[b] = silu(matmul(normed_b, win_ref[:, 3 * W :])).astype(BF16)
+
+    recv(tok_all.at[partner], s_tok)
+    send(tok_all.at[partner], tok_all.at[partner], s_tok + 2, hist_dev(sib))
+    recv(tok_all.at[sib], s_tok + 1)
+    keys_values(sib)
+    keys_values(partner)
 
     for o in range(1, ring):
         recv(nall.at[core, y, x_from(o)], s_n2x + o)
@@ -360,14 +368,21 @@
     s_n3y = slots(ring)
     s_n3x = slots(ring)
     s_iy = slots(1)
-    for o in range(1, ring):
+
+    def third_leg(o):
         send(nall.at[core, y], nall.at[core, y], s_n3y + o, y_dev(y_to(o)))
         send(nall.at[core, ring + x], nall.at[core, ring + x], s_n3x + o, x_dev(x_to(o)))
+
+    for o in (1, ring - 1)[: ring - 1]:
+        third_leg(o)
     if nyh > 1:
         send(idy.at[yh], idy.at[yh], s_iy, y_dev(lax.rem(yh + 1, nyh) * 2 + yl))
     s_sib = slots(2 * ring)
     for k, own in enumerate((y, ring + x)):
         send(nall.at[core, own], nall.at[core, own], s_sib + k * ring, hist_dev(sib))
+
+    recv(tok_all.at[cross], s_tok + 2)
+    keys_values(cross)
 
     lane = lax.broadcasted_iota(jnp.int32, (1, 128), 1)
     low = lane < 64
@@ -394,7 +409,10 @@
         attn[:, cols] = jnp.where(low, halves[0], halves[1]).astype(BF16)
         return carry
 
-    lax.fori_loop(0, HEADS // 2, forward_pair, 0)
+    lax.fori_loop(0, 1, forward_pair, 0)
+    for o in range(2, ring - 1):
+        third_leg(o)
+    lax.fori_loop(1, HEADS // 2, forward_pair, 0)
 
     for k in range(5, 9):
         loads[k].wait()
@@ -410,12 +428,6 @@
     pos_col = jnp.sum(y_hat * t_hat, -1, keepdims=True) / TEMP
     pos_row = jnp.broadcast_to(pos_col, (R, 128)).T[0:1, :]
 
-    for o in range(1, ring):
-        for k, (src, base) in enumerate(((y_from(o), s_n3y), (ring + x_from(o), s_n3x))):
-            recv(nall.at[core, src], base + o)
-            send(nall.at[core, src], nall.at[core, src], s_sib + k * ring + o, hist_dev(sib))
-    s_my = slots(1)
-    send(my_own, my_sib, s_my, hist_dev(sib))
     if nyh > 1:
         recv(idy.at[lax.rem(yh + 1, nyh)], s_iy)
     for a in range(nyh):
@@ -433,23 +445,35 @@
                     at = pl.ds((place * zh + k % zh) * NH, NH)
                     idb[chunk, at] = jnp.broadcast_to(rows[:, k : k + 1], (NH, 128))
                     lcb[chunk, at] = jnp.broadcast_to(rows[:, 8 + k : 9 + k], (NH, 128))
-    for o in range(ring):
-        recv(nall.at[other, y_from(o)], s_sib + o)
-        recv(nall.at[other, ring + x_from(o)], s_sib + ring + o)
 
     span = ring * zh * NH
     tid_row = tid_ref[...].astype(F32)
 
-    def logits_chunk(c, acc):
-        lg = inner_product(nall[0, c].reshape(span, 256), y_hat_b[:, :256]) + inner_product(
-            nall[1, c].reshape(span, 256), y_hat_b[:, 256:]
-        )
-        lg = lg * (1.0 / TEMP) - lcb[c]
-        value = jnp.where(idb[c] != tid_row, jnp.exp(lg), 0.0)
-        ex[c] = value
-        return acc + jnp.sum(value.reshape(span // 8, 8, 128), 0)
-
-    acc = lax.fori_loop(0, chunks, logits_chunk, jnp.zeros((8, 128), F32))
+    def hand_on(o):
+        for k, (src, base) in enumerate(((y_from(o), s_n3y), (ring + x_from(o), s_n3x))):
+            recv(nall.at[core, src], base + o)
+            send(nall.at[core, src], nall.at[core, src], s_sib + k * ring + o, hist_dev(sib))
+
+    def logits(o, acc):
+        for k, c in enumerate((y_from(o), ring + x_from(o))):
+            recv(nall.at[other, c], s_sib + k * ring + o)
+            lg = inner_product(nall[0, c].reshape(span, 256), y_hat_b[:, :256]) + inner_product(
+                nall[1, c].reshape(span, 256), y_hat_b[:, 256:]
+            )
+            lg = lg * (1.0 / TEMP) - lcb[c]
+            value = jnp.where(idb[c] != tid_row, jnp.exp(lg), 0.0)
+            ex[c] = value
+            acc = acc + jnp.sum(value.reshape(span // 8, 8, 128), 0)
+        return acc
+
+    order = [0, 1, 3, 2] if ring == 4 else list(range(ring))
+    acc = jnp.zeros((8, 128), F32)
+    for k in range(1, ring):
+        hand_on(order[k])
+        acc = logits(order[k - 1], acc)
+    s_my = slots(1)
+    send(my_own, my_sib, s_my, hist_dev(sib))
+    acc = logits(order[-1], acc)
     total = jnp.exp(pos_row) + jnp.sum(acc, 0, keepdims=True)
     position = h * R + lax.broadcasted_iota(jnp.int32, (1, 128), 1)
     valid = jnp.where(position < len_ref[0], 1.0, 0.0)
@@ -466,6 +490,8 @@
         return carry
 
     lax.fori_loop(0, chunks, grad_chunk, 0)
+    s_ng = slots(1)
+    send(ngs.at[other], nga, s_ng, hist_dev(sib))
     ng = ngo[...].reshape(dp_size * NB, 128).T
     d_hat = pg * t_hat + jnp.concatenate(
         [matmul(ng, nall[c].reshape(dp_size * NB, 256)) for c in range(2)], axis=1
@@ -474,11 +500,99 @@
     d_out_b = d_out.astype(BF16)
     d_mixed = inner_product(d_out_b, wout_ref[...])
     da_all[h] = norm_back(d_mixed * gate_f, attn_normed, attn_inv).astype(BF16)
-    s_da = slots(HIST)
+    s_da = slots(3)
+    send(da_all.at[h], da_all.at[h], s_da, hist_dev(partner))
+    send(da_all.at[h], da_all.at[h], s_da + 1, hist_dev(sib))
+
+    def leg1(group):
+        src, arrived = group[0], group[1]
+        base = slots(2 * ring)
+        for o in range(1, ring):
+            send(src.at[y_to(o)], arrived.at[0, o], base + o, y_dev(y_to(o)))
+            send(src.at[ring + x_to(o)], arrived.at[1, o], base + ring + o, x_dev(x_to(o)))
+        return base
+
+    def leg2(group, base):
+        src, arrived, mid, arrived2 = group[:4]
+        out = slots(2 * ring)
+        for part, own in enumerate((y, ring + x)):
+            total = src[own].astype(F32)
+            for o in range(1, ring):
+                recv(arrived.at[part, o], base + part * ring + o)
+                total = total + arrived[part, o].astype(F32)
+            mid[part] = total.astype(BF16).reshape(mid.shape[1:])
+            for o in range(1, ring):
+                to, device = (x_to(o), x_dev(x_to(o))) if part == 0 else (y_to(o), y_dev(y_to(o)))
+                send(mid.at[part, to], arrived2.at[part, o], out + part * ring + o, device)
+        return out
+
+    def leg3(group, base):
+        mid, arrived2, zs, zr = group[2:6]
+        for part, own in enumerate((x, y)):
+            total = mid[part, own].astype(F32)
+            for o in range(1, ring):
+                recv(arrived2.at[part, o], base + part * ring + o)
+                total = total + arrived2[part, o].astype(F32)
+            total = total.reshape((zh, total.shape[0] // zh, total.shape[1]))
+            if zs.dtype == BF16:
+                half = total.shape[2] // 2
+                total = jnp.concatenate([total[:, :, :half], total[:, :, half:]], axis=1).astype(BF16)
+            zs[part * zh : (part + 1) * zh] = total
+        out = slots(nz)
+        for o in range(1, nz):
+            send(zs.at[z_to(o)], zr.at[o], out + o, z_dev(z_to(o)))
+        return out
+
+    def leg4(group, base):
+        zs, zr, eh = group[4:]
+        total = zs[z].astype(F32)
+        for o in range(1, nz):
+            recv(zr.at[o], base + o)
+            total = total + zr[o].astype(F32)
+        if zs.dtype == BF16:
+            rows = total.shape[0] // 2
+            total = jnp.concatenate([total[:rows], total[rows:]], axis=1)
+        eh[h] = total
+        out = slots(HIST)
+        for o in range(1, HIST):
+            send(eh.at[h], eh.at[h], out + o, hist_dev(hist_to(o)))
+        return out
+
+    def arrive(group, base):
+        for o in range(1, HIST):
+            recv(group[6].at[hist_from(o)], base + o)
+
+    def spread(result, k, group, c0):
+        width = result.shape[1]
+        for a in range(nyh):
+            for b in range(nx):
+                for half in range(2):
+                    block = jnp.concatenate(
+                        [
+                            result[((half * zh + j) * npl + a * nx + b) * rw :][:rw]
+                            for j in range(zh)
+                        ],
+                        axis=0,
+                    ).astype(BF16)
+                    chunk, place = (2 * a + k, b) if half == 0 else (ring + b, 2 * a + k)
+                    group[0][chunk, place * zh * rw : (place + 1) * zh * rw, c0 : c0 + width] = block
+
     for o in range(1, HIST):
-        send(da_all.at[h], da_all.at[h], s_da + o, hist_dev(hist_to(o)))
-    s_ng = slots(1)
-    send(ngs.at[other], nga, s_ng, hist_dev(sib))
+        b = hist_from(o)
+        q_all[b] = silu(matmul(nrm_all[b], win_ref[:, 2 * W : 3 * W])).astype(BF16)
+
+    recv(my_sib, s_my)
+    recv(nga, s_ng)
+
+    def neg_chunk(c, carry):
+        left = jnp.concatenate([ngs[core, c], nga[c]], axis=1)
+        right = jnp.concatenate([my_own[:, W:], my_sib[:, W:]], axis=0)
+        g1[0][c] = matmul(left, right).astype(BF16)
+        return carry
+
+    lax.fori_loop(0, chunks, neg_chunk, 0)
+    t1 = leg1(g1)
+
     dout[...] = d_out
     dtgt_ref[...] = unit_back(pg * y_hat, t_hat, t_inv).astype(BF16)
     store(dtgt_ref, dtgt_hbm)
@@ -515,86 +629,31 @@
     s_dq = slots(1)
     send(dpq.at[other], dpq_r, s_dq, hist_dev(sib))
 
-    def leg1(group):
-        src, arrived = group[0], group[1]
-        base = slots(2 * ring)
-        for o in range(1, ring):
-            send(src.at[y_to(o)], arrived.at[0, o], base + o, y_dev(y_to(o)))
-            send(src.at[ring + x_to(o)], arrived.at[1, o], base + ring + o, x_dev(x_to(o)))
-        return base
-
-    def leg2(group, base):
-        src, arrived, mid, arrived2 = group[:4]
-        out = slots(2 * ring)
-        for part, own in enumerate((y, ring + x)):
-            total = src[own].astype(F32)
-            for o in range(1, ring):
-                recv(arrived.at[part, o], base + part * ring + o)
-                total = total + arrived[part, o].astype(F32)
-            mid[part] = total.astype(BF16).reshape(mid.shape[1:])
-            for o in range(1, ring):
-                to, device = (x_to(o), x_dev(x_to(o))) if part == 0 else (y_to(o), y_dev(y_to(o)))
-                send(mid.at[part, to], arrived2.at[part, o], out + part * ring + o, device)
-        return out
-
-    def leg3(group, base):
-        mid, arrived2, zs, zr = group[2:6]
-        for part, own in enumerate((x, y)):
-            total = mid[part, own].astype(F32)
-            for o in range(1, ring):
-                recv(arrived2.at[part, o], base + part * ring + o)
-                total = total + arrived2[part, o].astype(F32)
-            zs[part * zh : (part + 1) * zh] = total.reshape((zh,) + zs.shape[1:])
-        out = slots(nz)
-        for o in range(1, nz):
-            send(zs.at[z_to(o)], zr.at[o], out + o, z_dev(z_to(o)))
-        return out
-
-    def leg4(group, base):
-        zs, zr, eh = group[4:]
-        total = zs[z]
-        for o in range(1, nz):
-            recv(zr.at[o], base + o)
-            total = total + zr[o]
-        eh[h] = total
-        out = slots(HIST)
-        for o in range(1, HIST):
-            send(eh.at[h], eh.at[h], out + o, hist_dev(hist_to(o)))
-        return out
-
-    def arrive(group, base):
-        for o in range(1, HIST):
-            recv(group[6].at[hist_from(o)], base + o)
-
-    def spread(result, k, group, c0):
-        width = result.shape[1]
-        for a in range(nyh):
-            for b in range(nx):
-                for half in range(2):
-                    block = jnp.concatenate(
-                        [
-                            result[((half * zh + j) * npl + a * nx + b) * rw :][:rw]
-                            for j in range(zh)
-                        ],
-                        axis=0,
-                    ).astype(BF16)
-                    chunk, place = (2 * a + k, b) if half == 0 else (ring + b, 2 * a + k)
-                    group[0][chunk, place * zh * rw : (place + 1) * zh * rw, c0 : c0 + width] = block
-
-    recv(my_sib, s_my)
-    recv(nga, s_ng)
-
-    def neg_chunk(c, carry):
-        left = jnp.concatenate([ngs[core, c], nga[c]], axis=1)
-        right = jnp.concatenate([my_own[:, W:], my_sib[:, W:]], axis=0)
-        g1[0][c] = matmul(left, right).astype(BF16)
-        return carry
-
-    lax.fori_loop(0, chunks, neg_chunk, 0)
-    t1 = leg1(g1)
-
     mixed_t = jnp.concatenate([my_own[:, :W], my_sib[:, :W]], axis=0).T
     normed_t = jnp.concatenate([nrm_all[h], nrm_all[sib]], axis=0).T
+    causal_t = lax.broadcasted_iota(jnp.int32, (R, L), 1) >= h * R + lax.broadcasted_iota(
+        jnp.int32, (R, L), 0
+    )
+
+    def key_prepare(n, carry):
+        cols = pl.ds(pl.multiple_of(n * 128, 128), 128)
+        k = k_all[h, :, cols]
+        q = q_all[:, :, cols].reshape(L, 128)
+        for e in range(2):
+            s = inner_product(k * half_mask[e], q) * scale
+            sigma = sigmoid(s)
+            weights_t[2 * n + e] = jnp.where(causal_t, s * sigma * (1.0 / L), 0.0).astype(BF16)
+            slope_t[2 * n + e] = jnp.where(
+                causal_t, sigma * (1.0 + s * (1.0 - sigma)) * (scale / L), 0.0
+            )
+        for first in (W, 3 * W):
+            at = pl.ds(pl.multiple_of(first + n * 128, 128), 128)
+            proj[:, at] = silu_slope(proj[:, at])
+        return carry
+
+    lax.fori_loop(0, HEADS // 2, key_prepare, 0)
+    recv(da_all.at[partner], s_da)
+    send(da_all.at[partner], da_all.at[partner], s_da + 2, hist_dev(sib))
     recv(dpq_r, s_dq)
     for k in range(2):
         right = jnp.concatenate([dpq[core, k], dpq_r[k]], axis=0)
@@ -602,9 +661,6 @@
         spread(matmul(normed_t, right[:, 128:]), k, g2, 128)
     t2 = leg1(g2)
 
-    for o in range(1, HIST):
-        b = hist_from(o)
-        q_all[b] = silu(matmul(nrm_all[b], win_ref[:, 2 * W : 3 * W])).astype(BF16)
 
     for o in range(1, ring):
         recv(l1.at[x_from(o)], s_l1 + o)
@@ -616,33 +672,22 @@
     for o in range(1, ring):
         send(l2.at[y], l2.at[y], s_l2 + o, y_dev(y_to(o)))
 
-    for o in range(1, HIST):
-        recv(da_all.at[hist_from(o)], s_da + o)
-    causal_t = lax.broadcasted_iota(jnp.int32, (R, L), 1) >= h * R + lax.broadcasted_iota(
-        jnp.int32, (R, L), 0
-    )
-
+    recv(da_all.at[sib], s_da + 1)
+    recv(da_all.at[cross], s_da + 2)
     def key_pair(n, carry):
         cols = pl.ds(pl.multiple_of(n * 128, 128), 128)
-        k = k_all[h, :, cols]
         v = v_all[h, :, cols]
         q = q_all[:, :, cols].reshape(L, 128)
         da = da_all[:, :, cols].reshape(L, 128)
         dks, dvs = [], []
         for e in range(2):
-            s = inner_product(k * half_mask[e], q) * scale
-            sigma = sigmoid(s)
-            w = jnp.where(causal_t, s * sigma * (1.0 / L), 0.0).astype(BF16)
             dw = inner_product(v * half_mask[e], da)
-            ds = jnp.where(
-                causal_t, dw * (sigma * (1.0 + s * (1.0 - sigma))) * (scale / L), 0.0
-            ).astype(BF16)
-            dks.append(matmul(ds, q))
-            dvs.append(matmul(w, da))
+            dks.append(matmul((dw * slope_t[2 * n + e]).astype(BF16), q))
+            dvs.append(matmul(weights_t[2 * n + e], da))
         for at, parts, place in ((W, dvs, 0), (3 * W, dks, 128)):
             grad = jnp.where(low, parts[0], parts[1]).astype(BF16).astype(F32)
             at = pl.ds(pl.multiple_of(at + n * 128, 128), 128)
-            piece = (grad * silu_slope(proj[:, at])).astype(BF16)
+            piece = (grad * proj[:, at]).astype(BF16)
             dpo[:, at] = piece
             dpk[lax.rem(n, 2), lax.div(n, 2), :, place : place + 128] = piece
         return carry
@@ -658,6 +703,7 @@
         spread(matmul(normed_t, right), k, g3, 0)
     t3 = leg1(g3)
     t2 = leg2(g2, t2)
+    t1 = leg3(g1, t1)
 
     for o in range(1, ring):
         recv(l2.at[y_from(o)], s_l2 + o)
@@ -673,7 +719,6 @@
     dtok_ref[...] = (dout[...] + norm_back(grad, nrmf[...], inverse)).astype(BF16)
     store(dtok_ref, dtok_hbm)
 
-    t1 = leg3(g1, t1)
     t3 = leg2(g3, t3)
     t2 = leg3(g2, t2)
     t1 = leg4(g1, t1)
@@ -740,15 +785,16 @@
     vmem = pltpu.VMEM
     count = 256
 
-    def group(rows, width):
+    def group(rows, width, narrow):
         block = ring * zh * rows
+        over_z = vmem((nz, 2 * rows, width // 2), BF16) if narrow else vmem((nz, rows, width), F32)
         return (
             vmem((chunks, block, width), BF16),
             vmem((2, ring, block, width), BF16),
             vmem((2, ring, zh * rows, width), BF16),
             vmem((2, ring, zh * rows, width), BF16),
-            vmem((nz, rows, width), F32),
-            vmem((nz, rows, width), F32),
+            over_z,
+            over_z,
             vmem((HIST, rows, width), F32),
         )
 
@@ -777,6 +823,8 @@
         vmem((HIST, R, W), BF16),
         vmem((HIST, R, W), BF16),
         vmem((HEADS, R, L), F32),
+        vmem((HEADS, R, L), F32),
+        vmem((HEADS, R, L), BF16),
         vmem((R, W), BF16),
         vmem((2, chunks, ring, zh, NH, 256), BF16),
         vmem((nz, 8, 128), jnp.int32),
@@ -797,9 +845,9 @@
         vmem((2, R, 256), BF16),
         vmem((R, 4 * W), BF16),
         vmem((R, W), F32),
-        group(NQ, W),
-        group(rw, 384),
-        group(rw, 256),
+        group(NQ, W, True),
+        group(rw, 384, False),
+        group(rw, 256, True),
         vmem((ring, 8, 128), F32),
         vmem((ring, 8, 128), F32),
         vmem((nz, 8, 128), F32),

time: 75.3 us -> 71.6 us (0.951)
  Pallas kernels: 73.9 us -> 70.2 us
    pallas_call x1, Pallas kernels: 71.5 us -> 67.8 us  [local(): pl.pallas_call(functools.partial(kernel, sizes, count), out_shape=shapes,...]
where the time goes in v4:
time: 71.6 us; the launch traced here: 71.5 us
  Pallas kernels  70.2 us (98%)
  between operations  1.29 us (2%)
    pallas_call x1, Pallas kernels, local(): pl.pallas_call(functools.partial(kernel, sizes, count), out_shape=shapes,...  67.8 us
    pallas_call x1, Pallas kernels, local(): pl.pallas_call(hand_over, out_shape=shapes, in_specs=[pl.BlockSpec(memory...  2.35 us

profile of v4, /device:TPU:1, one launch (start us, length us, event | category | flops | bytes accessed | tf_op | source)
XLA Modules:
  0.0 71.5 jit_solution(16849026982579475492)
XLA Ops:
  1.3 67.8 %shard_map.136 = (f32[1,1]{1,0:T(1,128)}, bf16[128,512]{1,0:T(8,128)(2,1)}, bf16[128,512]{1,0:T(8,128)(2,1)}, f32[8,2048]{1,0:T(8,128)}, f32[8,512]{1,0:T(8,128)}, /*index=5*/f32[32,512]{1,0:T(8,128)}) custom-call(bf16[128,512]{1,0:T(8,128)(2,1)} %bitcast.7, bf16[128,512]{1,0:T(8,128)(2,1)} %bitcast.8, s32[1,128]{1,0:T(1,128)} %tid_hbm.1, ...), custom_call_target="tpu_custom_call" | custom-call | tf_op jit(solution)/shard_map/pallas_call | solution.py:869
  69.1 2.3 %shard_map.137 = (f32[1,1]{1,0:T(1,128)}, bf16[128,512]{1,0:T(8,128)(2,1)}, bf16[128,512]{1,0:T(8,128)(2,1)}, f32[8,2048]{1,0:T(8,128)}, f32[8,512]{1,0:T(8,128)}, /*index=5*/f32[32,512]{1,0:T(8,128)}) custom-call(f32[1,1]{1,0:T(1,128)} %get-tuple-element.18.refs_0_, bf16[128,512]{1,0:T(8,128)(2,1)} %get-tuple-element.19.refs_1_, ...), custom_call_target="tpu_custom_call" | custom-call | tf_op jit(solution)/shard_map/pallas_call | solution.py:889

commit v5 on v4

--- a/solution.py
+++ b/solution.py
@@ -138,6 +138,7 @@
     dpo,
     dout,
     g1,
+    gz,
     g2,
     g3,
     l1,
@@ -584,14 +585,73 @@
     recv(my_sib, s_my)
     recv(nga, s_ng)
 
-    def neg_chunk(c, carry):
+    right = jnp.concatenate([my_own[:, W:], my_sib[:, W:]], axis=0)
+    zsrc, zgot, amid, agot, bmid, bgot, ez = gz
+
+    def neg_chunk(c, part, index):
         left = jnp.concatenate([ngs[core, c], nga[c]], axis=1)
-        right = jnp.concatenate([my_own[:, W:], my_sib[:, W:]], axis=0)
-        g1[0][c] = matmul(left, right).astype(BF16)
-        return carry
-
-    lax.fori_loop(0, chunks, neg_chunk, 0)
-    t1 = leg1(g1)
+        result = matmul(left, right)
+        g1[0][c] = result[:, :256].astype(BF16)
+        for j in range(zh):
+            block = jnp.concatenate(
+                [result[(k * zh + j) * NQ : (k * zh + j + 1) * NQ, 256:] for k in range(ring)], axis=0
+            )
+            zsrc[part * zh + j, index] = block.astype(BF16)
+
+    t1 = slots(2 * ring)
+    for o in order[1:] + [0]:
+        for part, index in enumerate((y_to(o), x_to(o))):
+            c = part * ring + index
+            neg_chunk(c, part, index)
+            if o:
+                device = y_dev(index) if part == 0 else x_dev(index)
+                send(g1[0].at[c], g1[1].at[part, o], t1 + part * ring + o, device)
+    s_zz = slots(nz)
+    for o in range(1, nz):
+        send(zsrc.at[z_to(o)], zgot.at[o], s_zz + o, z_dev(z_to(o)))
+
+    def turn(low_index, high_index):
+        return low_index + upper * (high_index - low_index)
+
+    def turn_dev(low_dev, high_dev):
+        return {name: turn(low_dev[name], high_dev[name]) for name in ("dp", "hist")}
+
+    def z_first_leg2():
+        total = zsrc[z].astype(F32)
+        for o in range(1, nz):
+            recv(zgot.at[o], s_zz + o)
+            total = total + zgot[o].astype(F32)
+        amid[...] = total.astype(BF16)
+        out = slots(ring)
+        for o in range(1, ring):
+            to = turn(y_to(o), x_to(o))
+            send(amid.at[to], agot.at[o], out + o, turn_dev(y_dev(y_to(o)), x_dev(x_to(o))))
+        return out
+
+    def z_first_leg3(base):
+        total = amid[turn(y, x)].astype(F32)
+        for o in range(1, ring):
+            recv(agot.at[o], base + o)
+            total = total + agot[o].astype(F32)
+        total = total.reshape(ring, NQ, 256)
+        bmid[...] = jnp.concatenate([total[:, :, :128], total[:, :, 128:]], axis=1).astype(BF16)
+        out = slots(ring)
+        for o in range(1, ring):
+            to = turn(x_to(o), y_to(o))
+            send(bmid.at[to], bgot.at[o], out + o, turn_dev(x_dev(x_to(o)), y_dev(y_to(o))))
+        return out
+
+    def z_first_leg4(base):
+        total = bmid[turn(x, y)].astype(F32)
+        for o in range(1, ring):
+            recv(bgot.at[o], base + o)
+            total = total + bgot[o].astype(F32)
+        ez[h] = jnp.concatenate([total[:NQ], total[NQ:]], axis=1)
+        out = slots(HIST)
+        for o in range(1, HIST):
+            send(ez.at[h], ez.at[h], out + o, hist_dev(hist_to(o)))
+        return out
+
 
     dout[...] = d_out
     dtgt_ref[...] = unit_back(pg * y_hat, t_hat, t_inv).astype(BF16)
@@ -696,15 +756,13 @@
     s_dk = slots(1)
     send(dpk.at[other], dpk_r, s_dk, hist_dev(sib))
 
-    t1 = leg2(g1, t1)
     recv(dpk_r, s_dk)
     for k in range(2):
         right = jnp.concatenate([dpk[core, k], dpk_r[k]], axis=0)
         spread(matmul(normed_t, right), k, g3, 0)
     t3 = leg1(g3)
+    t1 = leg2(g1, t1)
     t2 = leg2(g2, t2)
-    t1 = leg3(g1, t1)
-
     for o in range(1, ring):
         recv(l2.at[y_from(o)], s_l2 + o)
     part = l2[0]
@@ -720,9 +778,11 @@
     store(dtok_ref, dtok_hbm)
 
     t3 = leg2(g3, t3)
+    tz = z_first_leg2()
+    t1 = leg3(g1, t1)
     t2 = leg3(g2, t2)
-    t1 = leg4(g1, t1)
     t3 = leg3(g3, t3)
+    tz = z_first_leg3(tz)
     for o in range(1, nz):
         recv(l3.at[z_from(o)], s_l3 + o)
     part = l3[0]
@@ -731,15 +791,19 @@
     l4[core] = part
     s_l4 = slots(1)
     send(l4.at[core], l4.at[core], s_l4, hist_dev(sib))
+    t1 = leg4(g1, t1)
     t2 = leg4(g2, t2)
-    arrive(g1, t1)
-    d_nhat = g1[6][...].reshape(NB, W)
-    dneg_ref[...] = unit_back(d_nhat, n_hat, n_inv) / total_events
-    store(dneg_ref, dneg_hbm)
+    tz = z_first_leg4(tz)
     t3 = leg4(g3, t3)
     recv(l4.at[other], s_l4)
     loss_ref[...] = (l4[0] + l4[1])[0:1, 0:1] / total_events
     store(loss_ref, loss_hbm)
+    arrive(g1, t1)
+    for o in range(1, HIST):
+        recv(ez.at[hist_from(o)], tz + o)
+    d_nhat = jnp.concatenate([g1[6][...].reshape(NB, 256), ez[...].reshape(NB, 256)], axis=1)
+    dneg_ref[...] = unit_back(d_nhat, n_hat, n_inv) / total_events
+    store(dneg_ref, dneg_hbm)
     arrive(g2, t2)
     for k in range(HIST):
         cols = slice(k * 128, (k + 1) * 128)
@@ -845,7 +909,16 @@
         vmem((2, R, 256), BF16),
         vmem((R, 4 * W), BF16),
         vmem((R, W), F32),
-        group(NQ, W, True),
+        group(NQ, 256, True),
+        (
+            vmem((nz, ring, ring * NQ, 256), BF16),
+            vmem((nz, ring, ring * NQ, 256), BF16),
+            vmem((ring, ring * NQ, 256), BF16),
+            vmem((ring, ring * NQ, 256), BF16),
+            vmem((ring, 2 * NQ, 128), BF16),
+            vmem((ring, 2 * NQ, 128), BF16),
+            vmem((HIST, NQ, 256), F32),
+        ),
         group(rw, 384, False),
         group(rw, 256, True),
         vmem((ring, 8, 128), F32),

time: 71.6 us -> 67.8 us (0.947)
  Pallas kernels: 70.2 us -> 66.4 us
    pallas_call x1, Pallas kernels: 67.8 us -> 64.1 us  [local(): pl.pallas_call(functools.partial(kernel, sizes, count), out_shape=shapes,...]
where the time goes in v5:
time: 67.8 us; the launch traced here: 67.7 us
  Pallas kernels  66.4 us (98%)
  between operations  1.29 us (2%)
    pallas_call x1, Pallas kernels, local(): pl.pallas_call(functools.partial(kernel, sizes, count), out_shape=shapes,...  64.1 us
    pallas_call x1, Pallas kernels, local(): pl.pallas_call(hand_over, out_shape=shapes, in_specs=[pl.BlockSpec(memory...  2.35 us

profile of v5, /device:TPU:1, one launch (start us, length us, event | category | flops | bytes accessed | tf_op | source)
XLA Modules:
  0.0 67.7 jit_solution(7552793868910706994)
XLA Ops:
  1.3 64.1 %shard_map.136 = (f32[1,1]{1,0:T(1,128)}, bf16[128,512]{1,0:T(8,128)(2,1)}, bf16[128,512]{1,0:T(8,128)(2,1)}, f32[8,2048]{1,0:T(8,128)}, f32[8,512]{1,0:T(8,128)}, /*index=5*/f32[32,512]{1,0:T(8,128)}) custom-call(bf16[128,512]{1,0:T(8,128)(2,1)} %bitcast.7, bf16[128,512]{1,0:T(8,128)(2,1)} %bitcast.8, s32[1,128]{1,0:T(1,128)} %tid_hbm.1, ...), custom_call_target="tpu_custom_call" | custom-call | tf_op jit(solution)/shard_map/pallas_call | solution.py:942
  65.4 2.3 %shard_map.137 = (f32[1,1]{1,0:T(1,128)}, bf16[128,512]{1,0:T(8,128)(2,1)}, bf16[128,512]{1,0:T(8,128)(2,1)}, f32[8,2048]{1,0:T(8,128)}, f32[8,512]{1,0:T(8,128)}, /*index=5*/f32[32,512]{1,0:T(8,128)}) custom-call(f32[1,1]{1,0:T(1,128)} %get-tuple-element.18.refs_0_, bf16[128,512]{1,0:T(8,128)(2,1)} %get-tuple-element.19.refs_1_, ...), custom_call_target="tpu_custom_call" | custom-call | tf_op jit(solution)/shard_map/pallas_call | solution.py:962

commit v6 on v5

--- a/solution.py
+++ b/solution.py
@@ -301,7 +301,7 @@
     s_nz = slots(nz)
     s_iz = slots(nz)
     own_slot = nall.at[core, own_chunk, own_place, own_z]
-    for o in range(1, nz):
+    for o in sorted(range(1, nz), key=lambda o: -min(o, nz - o)):
         send(own_slot, own_slot, s_nz + o, z_dev(z_to(o)))
         send(idz.at[z], idz.at[z], s_iz + o, z_dev(z_to(o)))
     s_tok = slots(3)
@@ -508,7 +508,7 @@
     def leg1(group):
         src, arrived = group[0], group[1]
         base = slots(2 * ring)
-        for o in range(1, ring):
+        for o in sorted(range(1, ring), key=lambda o: -min(o, ring - o)):
             send(src.at[y_to(o)], arrived.at[0, o], base + o, y_dev(y_to(o)))
             send(src.at[ring + x_to(o)], arrived.at[1, o], base + ring + o, x_dev(x_to(o)))
         return base
@@ -540,7 +540,7 @@
                 total = jnp.concatenate([total[:, :, :half], total[:, :, half:]], axis=1).astype(BF16)
             zs[part * zh : (part + 1) * zh] = total
         out = slots(nz)
-        for o in range(1, nz):
+        for o in sorted(range(1, nz), key=lambda o: -min(o, nz - o)):
             send(zs.at[z_to(o)], zr.at[o], out + o, z_dev(z_to(o)))
         return out
 
@@ -607,7 +607,7 @@
                 device = y_dev(index) if part == 0 else x_dev(index)
                 send(g1[0].at[c], g1[1].at[part, o], t1 + part * ring + o, device)
     s_zz = slots(nz)
-    for o in range(1, nz):
+    for o in sorted(range(1, nz), key=lambda o: -min(o, nz - o)):
         send(zsrc.at[z_to(o)], zgot.at[o], s_zz + o, z_dev(z_to(o)))
 
     def turn(low_index, high_index):
@@ -773,14 +773,13 @@
     for o in range(1, nz):
         send(l3.at[z], l3.at[z], s_l3 + o, z_dev(z_to(o)))
 
-    grad = inner_product(dpo[...], win_ref[...])
-    dtok_ref[...] = (dout[...] + norm_back(grad, nrmf[...], inverse)).astype(BF16)
-    store(dtok_ref, dtok_hbm)
-
     t3 = leg2(g3, t3)
     tz = z_first_leg2()
     t1 = leg3(g1, t1)
     t2 = leg3(g2, t2)
+    grad = inner_product(dpo[...], win_ref[...])
+    dtok_ref[...] = (dout[...] + norm_back(grad, nrmf[...], inverse)).astype(BF16)
+    store(dtok_ref, dtok_hbm)
     t3 = leg3(g3, t3)
     tz = z_first_leg3(tz)
     for o in range(1, nz):
@@ -811,6 +810,9 @@
         dwin_ref[:, cols] = g2[6][k, :, 128:256] / total_events
         dwin_ref[:, 2 * W + k * 128 : 2 * W + (k + 1) * 128] = g2[6][k, :, 256:384] / total_events
     store(dwout_ref, dwout_hbm)
+    for copy in sends:
+        copy.wait_send()
+    sends.clear()
     arrive(g3, t3)
     for k in range(HIST):
         dwin_ref[:, W + k * 128 : W + (k + 1) * 128] = g3[6][k, :, 0:128] / total_events

time: 67.8 us -> 67 us (0.988)
  Pallas kernels: 66.4 us -> 65.6 us
    pallas_call x1, Pallas kernels: 64.1 us -> 63.2 us  [local(): pl.pallas_call(functools.partial(kernel, sizes, count), out_shape=shapes,...]
where the time goes in v6:
time: 67 us; the launch traced here: 66.9 us
  Pallas kernels  65.6 us (98%)
  between operations  1.29 us (2%)
    pallas_call x1, Pallas kernels, local(): pl.pallas_call(functools.partial(kernel, sizes, count), out_shape=shapes,...  63.2 us
    pallas_call x1, Pallas kernels, local(): pl.pallas_call(hand_over, out_shape=shapes, in_specs=[pl.BlockSpec(memory...  2.35 us

profile of v6, /device:TPU:1, one launch (start us, length us, event | category | flops | bytes accessed | tf_op | source)
XLA Modules:
  0.0 66.9 jit_solution(17997596783072738637)
XLA Ops:
  1.3 63.2 %shard_map.136 = (f32[1,1]{1,0:T(1,128)}, bf16[128,512]{1,0:T(8,128)(2,1)}, bf16[128,512]{1,0:T(8,128)(2,1)}, f32[8,2048]{1,0:T(8,128)}, f32[8,512]{1,0:T(8,128)}, /*index=5*/f32[32,512]{1,0:T(8,128)}) custom-call(bf16[128,512]{1,0:T(8,128)(2,1)} %bitcast.7, bf16[128,512]{1,0:T(8,128)(2,1)} %bitcast.8, s32[1,128]{1,0:T(1,128)} %tid_hbm.1, ...), custom_call_target="tpu_custom_call" | custom-call | tf_op jit(solution)/shard_map/pallas_call | solution.py:944
  64.5 2.3 %shard_map.137 = (f32[1,1]{1,0:T(1,128)}, bf16[128,512]{1,0:T(8,128)(2,1)}, bf16[128,512]{1,0:T(8,128)(2,1)}, f32[8,2048]{1,0:T(8,128)}, f32[8,512]{1,0:T(8,128)}, /*index=5*/f32[32,512]{1,0:T(8,128)}) custom-call(f32[1,1]{1,0:T(1,128)} %get-tuple-element.18.refs_0_, bf16[128,512]{1,0:T(8,128)(2,1)} %get-tuple-element.19.refs_1_, ...), custom_call_target="tpu_custom_call" | custom-call | tf_op jit(solution)/shard_map/pallas_call | solution.py:964
